TPU v7x, 256 devices: a whole 4x4x8 slice. The times are simulated.
256 devices in a mesh: gx: 8 (over z), gy: 32 (over y, x, core).
Axes of the slice: x: 4, y: 4, z: 8, core: 2. Of those that a mesh axis runs over, the one named last changes fastest.
Arguments:
- tokens: bfloat16 [512, 8192], P('gy', 'gx'), may hold values from -6 to 6
- gate_projection_weight: bfloat16 [8192, 28672], P('gx', 'gy'), may hold values from -0.0625 to 0.0625
- upward_projection_weight: bfloat16 [8192, 28672], P('gx', 'gy'), may hold values from -0.0625 to 0.0625
- down_projection_weight: bfloat16 [28672, 8192], P('gy', 'gx'), may hold values from -0.03125 to 0.03125
- gate_adapter_input_map: bfloat16 [8192, 64], P('gx'), may hold values from -0.0625 to 0.0625
- up_adapter_input_map: bfloat16 [8192, 64], P('gx'), may hold values from -0.0625 to 0.0625
- down_adapter_input_map: bfloat16 [28672, 64], P('gy'), may hold values from -0.03125 to 0.03125
- gate_adapter_output_map: bfloat16 [64, 28672], P(None, 'gy'), may hold values from -0.75 to 0.75
- up_adapter_output_map: bfloat16 [64, 28672], P(None, 'gy'), may hold values from -0.75 to 0.75
- down_adapter_output_map: bfloat16 [64, 8192], P(None, 'gx'), may hold values from -0.75 to 0.75
- cotangent: bfloat16 [512, 8192], P('gy', 'gx'), may hold values from -6 to 6
Outputs:
- output: bfloat16 [512, 8192], P('gy', 'gx')
- token_input_gradient: bfloat16 [512, 8192], P('gy', 'gx')
- gate_output_map_gradient: float32 [64, 28672], P('gx', 'gy')
- up_output_map_gradient: float32 [64, 28672], P('gx', 'gy')
- down_output_map_gradient: float32 [64, 8192], P('gy', 'gx')
All inputs are finite; a program needn't handle non-finite values.
Results may differ from a plain program's by a relative error of at most 0.02.
Values may be sent and summed in bfloat16 or wider, within the bound.
A program may use at most 64 MiB of HBM per device.

v0:
```python
import jax
import jax.numpy as jnp
from jax import lax
from jax.sharding import PartitionSpec as P

adapter_scale = 0.5


def gated_product(left, right):
    return jnp.dot(left, right, preferred_element_type=jnp.float32)


def contract_trailing(left, right):
    return lax.dot_general(
        left, right, (((1,), (1,)), ((), ())), preferred_element_type=jnp.float32
    )


def contract_leading(left, right):
    return lax.dot_general(
        left, right, (((0,), (0,)), ((), ())), preferred_element_type=jnp.float32
    )


def body(
    tokens,
    gate_projection_weight,
    upward_projection_weight,
    down_projection_weight,
    gate_adapter_input_map,
    up_adapter_input_map,
    down_adapter_input_map,
    gate_adapter_output_map,
    up_adapter_output_map,
    down_adapter_output_map,
    cotangent,
):
    rank_width = gate_adapter_input_map.shape[1]
    rows_all = lax.all_gather(tokens, "gy", axis=0, tiled=True)
    gate_terms = gated_product(rows_all, gate_projection_weight)
    up_terms = gated_product(rows_all, upward_projection_weight)
    low_terms = gated_product(
        rows_all, jnp.concatenate([gate_adapter_input_map, up_adapter_input_map], axis=1)
    )
    gate_projection_sum, upward_projection_sum, low_sum = (
        lax.psum_scatter(gate_terms, "gx", scatter_dimension=0, tiled=True),
        lax.psum_scatter(up_terms, "gx", scatter_dimension=0, tiled=True),
        lax.psum_scatter(low_terms, "gx", scatter_dimension=0, tiled=True),
    )
    low_rank = low_sum.astype(jnp.bfloat16)
    gate_reduced = low_rank[:, :rank_width]
    upward_reduced = low_rank[:, rank_width:]
    gate_activation = gate_projection_sum + adapter_scale * gated_product(
        gate_reduced, gate_adapter_output_map
    )
    upward_activation = upward_projection_sum + adapter_scale * gated_product(
        upward_reduced, up_adapter_output_map
    )
    hidden_state = (jax.nn.silu(gate_activation) * upward_activation).astype(jnp.bfloat16)
    hidden_all = lax.all_gather(hidden_state, "gx", axis=0, tiled=True)
    out_terms = gated_product(hidden_all, down_projection_weight)
    down_terms = gated_product(hidden_all, down_adapter_input_map)
    output_total, down_sum = (
        lax.psum_scatter(out_terms, "gy", scatter_dimension=0, tiled=True),
        lax.psum_scatter(down_terms, "gy", scatter_dimension=0, tiled=True),
    )
    down_reduced = down_sum.astype(jnp.bfloat16)
    output = (
        output_total + adapter_scale * gated_product(down_reduced, down_adapter_output_map)
    ).astype(jnp.bfloat16)
    down_output_map_pieces = adapter_scale * contract_leading(down_reduced, cotangent)
    down_output_map_gradient = lax.psum_scatter(
        down_output_map_pieces.astype(jnp.bfloat16), "gy", scatter_dimension=0, tiled=True
    ).astype(jnp.float32)
    cot_all = lax.all_gather(cotangent, "gy", axis=0, tiled=True)
    grad_terms = contract_trailing(cot_all, down_projection_weight)
    back_terms = contract_trailing(cot_all, down_adapter_output_map)
    gradient_total, back_sum = (
        lax.psum_scatter(grad_terms, "gx", scatter_dimension=0, tiled=True),
        lax.psum_scatter(back_terms, "gx", scatter_dimension=0, tiled=True),
    )
    down_backward = back_sum.astype(jnp.bfloat16)
    hidden_gradient = gradient_total + adapter_scale * contract_trailing(
        down_backward, down_adapter_input_map
    )
    sigma = jax.nn.sigmoid(gate_activation)
    gate_gradient = (
        hidden_gradient * upward_activation * sigma * (1.0 + gate_activation * (1.0 - sigma))
    ).astype(jnp.bfloat16)
    upward_gradient = (hidden_gradient * gate_activation * sigma).astype(jnp.bfloat16)
    gate_gradient_pieces = adapter_scale * contract_leading(gate_reduced, gate_gradient)
    upward_gradient_pieces = adapter_scale * contract_leading(upward_reduced, upward_gradient)
    gate_output_map_gradient, up_output_map_gradient = (
        lax.psum_scatter(
            gate_gradient_pieces.astype(jnp.bfloat16), "gx", scatter_dimension=0, tiled=True
        ).astype(jnp.float32),
        lax.psum_scatter(
            upward_gradient_pieces.astype(jnp.bfloat16), "gx", scatter_dimension=0, tiled=True
        ).astype(jnp.float32),
    )
    gate_all, up_all = (
        lax.all_gather(gate_gradient, "gx", axis=0, tiled=True),
        lax.all_gather(upward_gradient, "gx", axis=0, tiled=True),
    )
    input_terms = contract_trailing(gate_all, gate_projection_weight) + contract_trailing(
        up_all, upward_projection_weight
    )
    back_low = jnp.concatenate(
        [
            contract_trailing(gate_all, gate_adapter_output_map),
            contract_trailing(up_all, up_adapter_output_map),
        ],
        axis=1,
    )
    input_total, rank_sum = (
        lax.psum_scatter(input_terms, "gy", scatter_dimension=0, tiled=True),
        lax.psum_scatter(back_low, "gy", scatter_dimension=0, tiled=True),
    )
    back_rank = rank_sum.astype(jnp.bfloat16)
    adapter_addend = contract_trailing(
        back_rank[:, :rank_width], gate_adapter_input_map
    ) + contract_trailing(back_rank[:, rank_width:], up_adapter_input_map)
    token_input_gradient = (input_total + adapter_scale * adapter_addend).astype(jnp.bfloat16)
    return (
        output,
        token_input_gradient,
        gate_output_map_gradient,
        up_output_map_gradient,
        down_output_map_gradient,
    )


def solution(mesh):
    in_specs = (
        P("gy", "gx"),
        P("gx", "gy"),
        P("gx", "gy"),
        P("gy", "gx"),
        P("gx", None),
        P("gx", None),
        P("gy", None),
        P(None, "gy"),
        P(None, "gy"),
        P(None, "gx"),
        P("gy", "gx"),
    )
    out_specs = (P("gy", "gx"), P("gy", "gx"), P("gx", "gy"), P("gx", "gy"), P("gy", "gx"))
    return jax.shard_map(body, mesh=mesh, in_specs=in_specs, out_specs=out_specs, check_vma=False)
```

profile of v0, /device:TPU:1, one launch (start us, length us, event | category | flops | bytes accessed | tf_op | source)
XLA Modules:
  0.0 944.2 jit_solution(16228319275529385304)
XLA Ops:
  8.7 53.9 %all-gather.3.cloned.1.call-done = bf16[512,1024]{1,0:T(8,128)(2,1)} async-done(((bf16[16,1024]{1,0:T(8,128)(2,1)}), bf16[512,1024]{1,0:T(8,128)(2,1)}) %all-gather.3.cloned.1.call-update) | async-done | bytes 1048592 | tf_op jit(solution)/shard_map/all_gather | solution.py:39
  62.6 1.9 convolution_bitcast_fusion
  65.5 4.0 fusion.26
  69.5 4.0 fusion.25
  73.6 38.8 %all-gather.5.cloned.1.call-done = bf16[512,1024]{1,0:T(8,128)(2,1)} async-done(((bf16[16,1024]{1,0:T(8,128)(2,1)}), bf16[512,1024]{1,0:T(8,128)(2,1)}) %all-gather.5.cloned.1.call-update) | async-done | bytes 1048592 | tf_op jit(solution)/shard_map/all_gather | solution.py:75
  112.4 2.4 fusion.30
  114.8 3.8 fusion.29
  118.7 26.7 %reduce-scatter.28.cloned.1.call-done = f32[64,128]{1,0:T(8,128)} async-done(((f32[512,128]{1,0:T(8,128)}), f32[64,128]{1,0:T(8,128)}) %reduce-scatter.28.cloned.1.call-update) | async-done | bytes 32784
  146.2 42.3 %reduce-scatter.16.cloned.1.call-done = f32[64,896]{1,0:T(8,128)} async-done(((f32[512,896]{1,0:T(8,128)}), f32[64,896]{1,0:T(8,128)}) %reduce-scatter.16.cloned.1.call-update) | async-done | bytes 229392 | tf_op jit(solution)/shard_map/reduce_scatter | solution.py:47
  188.5 1.1 fusion.1
  189.7 41.4 %reduce-scatter.14.cloned.1.call-done = f32[64,896]{1,0:T(8,128)} async-done(((f32[512,896]{1,0:T(8,128)}), f32[64,896]{1,0:T(8,128)}) %reduce-scatter.14.cloned.1.call-update) | async-done | bytes 229392 | tf_op jit(solution)/shard_map/reduce_scatter | solution.py:46
  232.2 35.8 %reduce-scatter.24.cloned.1.call-done = f32[64,64]{1,0:T(8,128)} async-done(((f32[512,64]{1,0:T(8,128)}), f32[64,64]{1,0:T(8,128)}) %reduce-scatter.24.cloned.1.call-update) | async-done | bytes 16400 | tf_op jit(solution)/shard_map/reduce_scatter | solution.py:80
  268.0 43.7 %reduce-scatter.22.cloned.1.call-done = f32[64,896]{1,0:T(8,128)} async-done(((f32[512,896]{1,0:T(8,128)}), f32[64,896]{1,0:T(8,128)}) %reduce-scatter.22.cloned.1.call-update) | async-done | bytes 229392 | tf_op jit(solution)/shard_map/reduce_scatter | solution.py:79
  311.7 1.2 multiply_convert_fusion
  313.7 20.8 %all_gather.18 = bf16[512,896]{1,0:T(8,128)(2,1)S(1)} all-gather(bf16[64,896]{1,0:T(8,128)(2,1)S(1)} %get-tuple-element.8), channel_id=1, replica_groups=mesh['gx'=8,'gy'=32] {'gx'}, dimensions={0}, use_global_device_ids=true | all-gather | bytes 1032192 | tf_op jit(solution)/shard_map/all_gather | solution.py:102
  334.9 22.8 %all_gather.19 = bf16[512,896]{1,0:T(8,128)(2,1)} all-gather(bf16[64,896]{1,0:T(8,128)(2,1)S(1)} %get-tuple-element.7), channel_id=1, replica_groups=mesh['gx'=8,'gy'=32] {'gx'}, dimensions={0}, use_global_device_ids=true | all-gather | bytes 1032192 | tf_op jit(solution)/shard_map/all_gather | solution.py:103
  357.7 21.1 %all_gather.16 = bf16[512,896]{1,0:T(8,128)(2,1)S(1)} all-gather(bf16[64,896]{1,0:T(8,128)(2,1)S(1)} %get-tuple-element.9), channel_id=1, replica_groups=mesh['gx'=8,'gy'=32] {'gx'}, dimensions={0}, use_global_device_ids=true | all-gather | bytes 1032192 | tf_op jit(solution)/shard_map/all_gather | solution.py:60
  380.9 1.6 fusion.33
  382.5 99.8 %reduce-scatter.20.cloned.1.call-done = f32[16,64]{1,0:T(8,128)} async-done(((f32[512,64]{1,0:T(8,128)}), f32[16,64]{1,0:T(8,128)}) %reduce-scatter.20.cloned.1.call-update) | async-done | bytes 4112 | tf_op jit(solution)/shard_map/reduce_scatter | solution.py:65
  482.3 1.6 fusion.3
  484.9 2.6 fusion.27
  488.7 2.9 fusion.31
  491.6 2.6 convolution_add_fusion
  497.3 56.5 %all-reduce.9.cloned.1.call-done = (bf16[64,896]{1,0:T(8,128)(2,1)}, bf16[64,896]{1,0:T(8,128)(2,1)}) async-done(((bf16[64,896]{1,0:T(8,128)(2,1)}, bf16[64,896]{1,0:T(8,128)(2,1)}), (bf16[64,896]{1,0:T(8,128)(2,1)}, bf16[64,896]{1,0:T(8,128)(2,1)})) %all-reduce.9.cloned.1.call-update) | async-done | bytes 229392
  553.9 1.4 dynamic-slice_convert_fusion
  555.2 115.1 %all-reduce.7.cloned.1.call-done = bf16[64,1024]{1,0:T(8,128)(2,1)} async-done(((bf16[64,1024]{1,0:T(8,128)(2,1)}), bf16[64,1024]{1,0:T(8,128)(2,1)}) %all-reduce.7.cloned.1.call-update) | async-done | bytes 131088
  670.3 1.3 dynamic-slice_convert_fusion.2
  671.6 84.7 %reduce-scatter.30.cloned.1.call-done = f32[16,128]{1,0:T(8,128)} async-done(((f32[512,128]{1,0:T(8,128)}), f32[16,128]{1,0:T(8,128)}) %reduce-scatter.30.cloned.1.call-update) | async-done | bytes 8208
  757.3 89.0 %reduce-scatter.18.cloned.1.call-done = f32[16,1024]{1,0:T(8,128)} async-done(((f32[512,1024]{1,0:T(8,128)}), f32[16,1024]{1,0:T(8,128)}) %reduce-scatter.18.cloned.1.call-update) | async-done | bytes 65552 | tf_op jit(solution)/shard_map/reduce_scatter | solution.py:64
  846.3 1.6 fusion.9
  847.9 88.1 %reduce-scatter.26.cloned.1.call-done = f32[16,1024]{1,0:T(8,128)} async-done(((f32[512,1024]{1,0:T(8,128)}), f32[16,1024]{1,0:T(8,128)}) %reduce-scatter.26.cloned.1.call-update) | async-done | bytes 65552 | tf_op jit(solution)/shard_map/reduce_scatter | solution.py:116
  936.0 1.6 fusion.10
  (71 shorter events, 12.9 us)
Async XLA Ops:
  7.2 107.7 %copy-start = (bf16[896,1024]{1,0:T(8,128)(2,1)S(1)}, bf16[896,1024]{1,0:T(8,128)(2,1)}, u32[]{:S(2)}) copy-start(bf16[896,1024]{1,0:T(8,128)(2,1)} %param.14) | copy-start | bytes 5505028
  7.2 55.4 %all-gather.3.cloned.1.call-start = ((), (), s32[]{:S(2)}) async-start(), calls=%async_computation.9 | async-start | bytes 1081344 | tf_op jit(solution)/shard_map/all_gather | solution.py:39
  7.9 104.5 %all-gather.5.cloned.1.call-start = ((), (), s32[]{:S(2)}) async-start(), calls=%async_computation.14 | async-start | bytes 1081344 | tf_op jit(solution)/shard_map/all_gather | solution.py:75
  8.7 136.7 %reduce-scatter.28.cloned.1.call-start = ((), (), s32[]{:S(2)}) async-start(), calls=%async_computation.18 | async-start | bytes 294912
  62.6 2.8 copy-start.4
  65.4 123.1 %reduce-scatter.16.cloned.1.call-start = ((), (), s32[]{:S(2)}) async-start(), calls=%async_computation.11 | async-start | bytes 2064384 | tf_op jit(solution)/shard_map/reduce_scatter | solution.py:47
  69.5 161.6 %reduce-scatter.14.cloned.1.call-start = ((), (), s32[]{:S(2)}) async-start(), calls=%async_computation.10 | async-start | bytes 2064384 | tf_op jit(solution)/shard_map/reduce_scatter | solution.py:46
  73.5 38.9 %copy-start.7 = (bf16[64,1024]{1,0:T(8,128)(2,1)S(1)}, bf16[64,1024]{1,0:T(8,128)(2,1)}, u32[]{:S(2)}) copy-start(bf16[64,1024]{1,0:T(8,128)(2,1)} %param.20) | copy-start | bytes 393220
  73.6 194.4 %reduce-scatter.24.cloned.1.call-start = ((), (), s32[]{:S(2)}) async-start(), calls=%async_computation.16 | async-start | bytes 294912 | tf_op jit(solution)/shard_map/reduce_scatter | solution.py:80
  114.8 196.9 %reduce-scatter.22.cloned.1.call-start = ((), (), s32[]{:S(2)}) async-start(), calls=%async_computation.15 | async-start | bytes 2064384 | tf_op jit(solution)/shard_map/reduce_scatter | solution.py:79
  118.6 69.9 %copy-start.9 = (bf16[64,896]{1,0:T(8,128)(2,1)S(1)}, bf16[64,896]{1,0:T(8,128)(2,1)}, u32[]{:S(2)}) copy-start(bf16[64,896]{1,0:T(8,128)(2,1)} %param.19) | copy-start | bytes 344068
  118.6 112.4 %copy-start.8 = (bf16[64,896]{1,0:T(8,128)(2,1)S(1)}, bf16[64,896]{1,0:T(8,128)(2,1)}, u32[]{:S(2)}) copy-start(bf16[64,896]{1,0:T(8,128)(2,1)} %param.18) | copy-start | bytes 344068
  118.6 193.1 %copy-start.11 = (bf16[896,64]{0,1:T(8,128)(2,1)S(1)}, bf16[896,64]{0,1:T(8,128)(2,1)}, u32[]{:S(2)}) copy-start(bf16[896,64]{0,1:T(8,128)(2,1)} %param.17) | copy-start | bytes 344068
  118.6 363.7 %reduce-scatter.20.cloned.1.call-start = ((), (), s32[]{:S(2)}) async-start(), calls=%async_computation.13 | async-start | bytes 270336 | tf_op jit(solution)/shard_map/reduce_scatter | solution.py:65
  334.5 23.2 %copy-start.1 = (bf16[512,896]{1,0:T(8,128)(2,1)}, bf16[512,896]{1,0:T(8,128)(2,1)S(1)}, u32[]{:S(2)}) copy-start(bf16[512,896]{1,0:T(8,128)(2,1)S(1)} %all_gather.18) | copy-start | bytes 2752516
  378.9 103.5 %copy-start.10 = (bf16[16,1024]{1,0:T(8,128)(2,1)S(1)}, bf16[16,1024]{1,0:T(8,128)(2,1)}, u32[]{:S(2)}) copy-start(bf16[16,1024]{1,0:T(8,128)(2,1)} %param.21) | copy-start | bytes 98308
  380.0 173.9 %all-reduce.9.cloned.1.call-start = ((), (), s32[]{:S(2)}) async-start(), calls=%async_computation.21 | async-start | bytes 458752
  380.9 289.4 %all-reduce.7.cloned.1.call-start = ((), (), s32[]{:S(2)}) async-start(), calls=%async_computation.20 | async-start | bytes 262144
  483.9 272.4 %reduce-scatter.30.cloned.1.call-start = ((), (), s32[]{:S(2)}) async-start(), calls=%async_computation.19 | async-start | bytes 270336
  484.8 361.4 %reduce-scatter.18.cloned.1.call-start = ((), (), s32[]{:S(2)}) async-start(), calls=%async_computation.12 | async-start | bytes 2162688 | tf_op jit(solution)/shard_map/reduce_scatter | solution.py:64
  487.5 1.2 copy-start.2
  487.5 448.5 %reduce-scatter.26.cloned.1.call-start = ((), (), s32[]{:S(2)}) async-start(), calls=%async_computation.17 | async-start | bytes 2162688 | tf_op jit(solution)/shard_map/reduce_scatter | solution.py:116
  488.7 2.9 copy-start.3
  488.7 2.9 copy-start.13
  494.2 0.7 copy-start.15
  494.2 1.3 copy-start.14
  494.2 262.9 %copy-start.6 = (bf16[1024,64]{0,1:T(8,128)(2,1)S(1)}, bf16[1024,64]{0,1:T(8,128)(2,1)}, u32[]{:S(2)}) copy-start(bf16[1024,64]{0,1:T(8,128)(2,1)} %param.15) | copy-start | bytes 393220
  494.2 352.1 %copy-start.12 = (f32[16,64]{1,0:T(8,128)S(1)}, f32[16,64]{1,0:T(8,128)}, u32[]{:S(2)}) copy-start(f32[16,64]{1,0:T(8,128)} %reduce-scatter.20.cloned.1.call-done) | copy-start | bytes 12292
  494.2 441.8 %copy-start.5 = (bf16[1024,64]{0,1:T(8,128)(2,1)S(1)}, bf16[1024,64]{0,1:T(8,128)(2,1)}, u32[]{:S(2)}) copy-start(bf16[1024,64]{0,1:T(8,128)(2,1)} %param.16) | copy-start | bytes 393220
Sparse Core Ops, SparseCore 0:
  10.6 52.0 all-gather.2
  65.2 47.1 all-gather.4
  114.9 30.3 reduce-scatter.27
  147.9 40.5 reduce-scatter.15
  191.1 39.9 reduce-scatter.13
  233.5 34.4 reduce-scatter.23
  270.6 41.0 reduce-scatter.21
  380.1 102.1 reduce-scatter.19
  484.7 69.1 all-reduce.8
  557.3 112.9 all-reduce.6
  674.0 82.2 reduce-scatter.29
  760.0 86.2 reduce-scatter.17
  850.1 85.8 reduce-scatter.25
where the time goes:
time: 945 us; the launch traced here: 944 us
  waiting for transfers between devices  817 us (86%)
  blocking collectives  64.8 us (7%)
  matrix products  37.2 us (4%)
  between operations  15.3 us (2%)
    unnamed x17, waiting for transfers between devices  284 us
    reduce_scatter x1, waiting for transfers between devices, body(): lax.psum_scatter(down_terms, 'gy', scatter_dimension=0, tiled=True)  99.8 us
    reduce_scatter x1, waiting for transfers between devices, body(): lax.psum_scatter(out_terms, 'gy', scatter_dimension=0, tiled=True)  89 us
    reduce_scatter x1, waiting for transfers between devices, body(): lax.psum_scatter(input_terms, 'gy', scatter_dimension=0, tiled=True)  88.1 us
    all_gather x1, waiting for transfers between devices, body(): rows_all = lax.all_gather(tokens, 'gy', axis=0, tiled=True)  53.9 us
    reduce_scatter x1, waiting for transfers between devices, body(): lax.psum_scatter(grad_terms, 'gx', scatter_dimension=0, tiled=True)  43.7 us
    reduce_scatter x1, waiting for transfers between devices, body(): lax.psum_scatter(up_terms, 'gx', scatter_dimension=0, tiled=True)  42.3 us
    reduce_scatter x1, waiting for transfers between devices, body(): lax.psum_scatter(gate_terms, 'gx', scatter_dimension=0, tiled=True)  41.4 us
  transfers between devices with their start and end apart: 13, of which 13 were waited for; matrix products, arithmetic and copies ran while one was open for 4% of the time, Pallas kernels for 0%

commit v1 on v0

v1 whole, which is shorter than its diff:
```python
import functools

import jax
import jax.numpy as jnp
from jax import lax
from jax.experimental import pallas as pl
from jax.experimental.pallas import tpu as pltpu
from jax.sharding import PartitionSpec as P

MESH = pl.DeviceIdType.MESH
F32 = jnp.float32
BF16 = jnp.bfloat16

NZ = 8
NG = 32
SIDE = 4
NC = 16
TB = 16
CH = 64
D = 1024
FF = 896
R = 64
W = D + 128
SCALE = 0.5


def nn(left, right):
    return jnp.dot(left, right, preferred_element_type=F32)


def nt(left, right):
    return lax.dot_general(left, right, (((1,), (1,)), ((), ())), preferred_element_type=F32)


def tn(left, right):
    return lax.dot_general(left, right, (((0,), (0,)), ((), ())), preferred_element_type=F32)


def kernel(
    tok, wg, wu, wd, ag, au, ad, bg, bu, bd, cot,
    out, tig, gmap, umap, dmap,
    X, VG, VU, VD, AG, AU, AD, BGU, BD,
    LZ, LA, DL, PG, PU, PH, GA, UA, RS, RR, H, ST, SB, O2, RX, LOWF,
    wsem, xsem, xs, xr, ys, yr, lzs, lzr, las, lar, dls, dlr, rss, rsr, ags, agr, sbs, sbr, rxs, rxr,
):
    z = lax.axis_index("gx")
    g = lax.axis_index("gy")
    q, c = g // 2, g % 2
    qx, qy = q % SIDE, q // SIDE
    sibling = g + 1 - 2 * c
    right, left = (z + 1) % NZ, (z + NZ - 1) % NZ

    def slot_of(qq, cc):
        return ((qq // 2 + 4 * cc) % NZ) * 4 + 2 * cc + qq % 2

    def chip_at(k, sign):
        dx, dy = k % SIDE, k // SIDE
        return ((qy + SIDE + sign * dy) % SIDE) * SIDE + (qx + SIDE + sign * dx) % SIDE

    def remote(src, dst, ssem, rsem, zz, gg):
        return pltpu.make_async_remote_copy(
            src_ref=src, dst_ref=dst, send_sem=ssem, recv_sem=rsem, device_id=(zz, gg), device_id_type=MESH
        )

    me = slot_of(q, c)

    own_copies = [
        pltpu.make_async_copy(tok, X.at[0, me], xsem.at[0]),
        pltpu.make_async_copy(cot, X.at[1, me], xsem.at[1]),
    ]
    low_copies = [
        pltpu.make_async_copy(ag, AG, wsem.at[0]),
        pltpu.make_async_copy(au, AU, wsem.at[1]),
        pltpu.make_async_copy(bd, BD, wsem.at[2]),
    ]
    gate_copies = [
        pltpu.make_async_copy(wg, VG, wsem.at[3]),
        pltpu.make_async_copy(wu, VU, wsem.at[4]),
    ]
    rest_copies = [
        pltpu.make_async_copy(wd, VD, wsem.at[5]),
        pltpu.make_async_copy(ad, AD, wsem.at[6]),
        pltpu.make_async_copy(bg, BGU.at[pl.ds(0, R)], wsem.at[7]),
        pltpu.make_async_copy(bu, BGU.at[pl.ds(R, R)], wsem.at[8]),
    ]
    for copy in own_copies + low_copies + gate_copies + rest_copies:
        copy.start()

    barrier = pltpu.get_barrier_semaphore()

    @pl.loop(1, NG)
    def _(k):
        pl.semaphore_signal(barrier, inc=1, device_id=(z, (g + k) % NG), device_id_type=MESH)

    @pl.loop(1, NZ)
    def _(k):
        pl.semaphore_signal(barrier, inc=1, device_id=((z + k) % NZ, g), device_id_type=MESH)

    zero_half = jnp.zeros((3, CH // 2, FF), BF16)
    RR[:, 0, 3, CH // 2 : CH, :] = zero_half
    RR[:, 1, 3, 0 : CH // 2, :] = zero_half
    RR[:, :, 4] = jnp.zeros((3, 2, CH, FF), BF16)
    LZ[z] = jnp.zeros((3 * TB, 128), BF16)
    DL[me] = jnp.zeros((TB, 128), BF16)

    for copy in own_copies:
        copy.wait()
    pl.semaphore_wait(barrier, NG - 1 + NZ - 1)

    def spread_send(a):
        remote(X.at[a, me], X.at[a, me], ys.at[a, 0], yr.at[a, 0], z, sibling).start()

        @pl.loop(1, NC)
        def _(k):
            remote(X.at[a, me], X.at[a, me], xs.at[a, k], xr.at[a, k], z, 2 * chip_at(k, 1) + c).start()

    def spread_relay(a):
        @pl.loop(1, NC)
        def _(k):
            s = slot_of(chip_at(k, -1), c)
            remote(X.at[a, s], X.at[a, s], xs.at[a, k], xr.at[a, k], z, sibling).wait_recv()
            remote(X.at[a, s], X.at[a, s], ys.at[a, k], yr.at[a, k], z, sibling).start()

        @pl.loop(0, NC)
        def _(k):
            s = slot_of(chip_at(k, -1), 1 - c)
            remote(X.at[a, s], X.at[a, s], ys.at[a, k], yr.at[a, k], z, sibling).wait_recv()

    spread_send(0)

    for copy in low_copies:
        copy.wait()
    LZ[z, 0:TB, 0:R] = nn(X[0, me], AG[...]).astype(BF16)
    LZ[z, TB : 2 * TB, 0:R] = nn(X[0, me], AU[...]).astype(BF16)
    LZ[z, 2 * TB : 3 * TB, 0:R] = nt(X[1, me], BD[...]).astype(BF16)

    @pl.loop(1, NZ)
    def _(k):
        remote(LZ.at[z], LZ.at[z], lzs.at[k], lzr.at[k], (z + k) % NZ, g).start()

    spread_relay(0)
    spread_send(1)

    @pl.loop(1, NZ)
    def _(k):
        s = (z + NZ - k) % NZ
        remote(LZ.at[s], LZ.at[s], lzs.at[k], lzr.at[k], z, g).wait_recv()

    LA[me] = jnp.sum(LZ[...].astype(F32), axis=0).astype(BF16)

    @pl.loop(1, NG)
    def _(k):
        remote(LA.at[me], LA.at[me], las.at[k], lar.at[k], z, (g + k) % NG).start()

    def low_wait():
        @pl.loop(1, NG)
        def _(k):
            p = (g + NG - k) % NG
            s = slot_of(p // 2, p % 2)
            remote(LA.at[s], LA.at[s], las.at[k], lar.at[k], z, g).wait_recv()

    for copy in gate_copies + rest_copies:
        copy.wait()

    def ring_copy(a, way, j, half):
        rows = pl.ds(way * (CH // 2), CH // 2) if half else pl.ds(0, CH)
        return remote(
            RS.at[a, way, j - 1, rows], RR.at[a, way, j - 1, rows],
            rss.at[a, way, j - 1], rsr.at[a, way, j - 1], left if way else right, g,
        )

    def ring_wait(a, j):
        @pl.when(j == 3)
        def _():
            ring_copy(a, 0, 4, True).wait_recv()
            ring_copy(a, 1, 4, True).wait_recv()

        @pl.when(j < 3)
        def _():
            ring_copy(a, 0, j + 1, False).wait_recv()
            ring_copy(a, 1, j + 1, False).wait_recv()

    def pair(ref, a, j):
        da, db = (z + j) % NZ, (z + NZ - j) % NZ
        xa = ref[a, pl.ds(4 * da, 4)].reshape(CH, D)
        xb = ref[a, pl.ds(4 * db, 4)].reshape(CH, D)
        return jnp.concatenate([xa, xb], axis=0)

    def ring_step(a, part, j):
        ring_wait(a, j)

        @pl.when(j > 0)
        def _():
            RS[a, 0, j - 1] = (part[0:CH] + RR[a, 0, j].astype(F32)).astype(BF16)
            RS[a, 1, j - 1] = (part[CH : 2 * CH] + RR[a, 1, j].astype(F32)).astype(BF16)

        @pl.when(j == 4)
        def _():
            ring_copy(a, 0, 4, True).start()
            ring_copy(a, 1, 4, True).start()

        @pl.when((j > 0) & (j < 4))
        def _():
            ring_copy(a, 0, j, False).start()
            ring_copy(a, 1, j, False).start()

    def ring_total(a, part):
        return part[0:CH] + (RR[a, 0, 0].astype(F32) + RR[a, 1, 0].astype(F32))

    def low_chunk(which):
        return LA[pl.ds(4 * z, 4), which * TB : (which + 1) * TB, :].reshape(CH, 128)[:, 0:R]

    def chain_copy(b, way, j, half, arriving):
        hops = j if arriving else j - 1
        d = (z + hops) % NZ if way else (z + NZ - hops) % NZ
        rows = pl.ds(way * (CH // 2), CH // 2) if half else pl.ds(0, CH)
        return remote(
            H.at[b, d, rows], H.at[b, d, rows],
            ags.at[b, way, j - 1], agr.at[b, way, j - 1], left if way else right, g,
        )

    def chain_start(b, j):
        @pl.when(j == 4)
        def _():
            chain_copy(b, 0, 4, True, False).start()
            chain_copy(b, 1, 4, True, False).start()

        @pl.when(j < 4)
        def _():
            chain_copy(b, 0, j, False, False).start()
            chain_copy(b, 1, j, False, False).start()

    def chain_wait(b, j):
        @pl.when(j == 4)
        def _():
            chain_copy(b, 0, 4, True, True).wait_recv()
            chain_copy(b, 1, 4, True, True).wait_recv()

        @pl.when((j > 0) & (j < 4))
        def _():
            chain_copy(b, 0, j, False, True).wait_recv()
            chain_copy(b, 1, j, False, True).wait_recv()

    @pl.loop(0, 6)
    def _(i):
        @pl.when(i < 5)
        def _():
            j = 4 - i
            x = pair(X, 0, j)
            PG[...] = nn(x, VG[...])
            ring_step(0, PG, j)
            PU[...] = nn(x, VU[...])
            ring_step(1, PU, j)

            @pl.when(j == 0)
            def _():
                low_wait()
                gate = ring_total(0, PG) + SCALE * nn(low_chunk(0), BGU[0:R])
                up = ring_total(1, PU) + SCALE * nn(low_chunk(1), BGU[R : 2 * R])
                GA[...] = gate
                UA[...] = up
                H[0, z] = (gate * jax.nn.sigmoid(gate) * up).astype(BF16)
                chain_start(0, 1)

        @pl.when(i == 1)
        def _():
            spread_relay(1)

        @pl.when(i > 0)
        def _():
            j = 5 - i
            PH[...] = nt(pair(X, 1, j), VD[...])
            ring_step(2, PH, j)

            @pl.when(j == 0)
            def _():
                grad = ring_total(2, PH) + SCALE * nt(low_chunk(2), AD[...])
                gate, up = GA[...], UA[...]
                sigma = jax.nn.sigmoid(gate)
                H[1, z] = (grad * up * sigma * (1.0 + gate * (1.0 - sigma))).astype(BF16)
                H[2, z] = (grad * gate * sigma).astype(BF16)
                chain_start(1, 1)
                chain_start(2, 1)

    def sib_copy(f, d):
        rows = pl.ds(pl.multiple_of((1 - c) * 32, 32), 32)
        return remote(ST.at[f, d, rows], SB.at[f, d], sbs.at[f, d], sbr.at[f, d], z, sibling)

    def sib_start(f, j):
        da, db = (z + NZ - j) % NZ, (z + j) % NZ
        sib_copy(f, da).start()

        @pl.when((j > 0) & (j < 4))
        def _():
            sib_copy(f, db).start()

    def owner_chip(d, k):
        return 2 * ((d + 4 * c) % NZ) + k

    def owner_copy(f, d, k):
        return remote(
            O2.at[f, d, pl.ds(k * TB, TB)], RX.at[f, q], rxs.at[f, 2 * d + k], rxr.at[f, q],
            z, 2 * owner_chip(d, k) + c,
        )

    def combine_one(f, d):
        sib_copy(f, d).wait_recv()
        rows = pl.ds(pl.multiple_of(c * 32, 32), 32)
        total = (ST[f, d, rows].astype(F32) + SB[f, d].astype(F32)).astype(BF16)
        O2[f, d] = total
        for k in range(2):
            own = owner_chip(d, k) == q

            @pl.when(own)
            def _():
                RX[f, q] = total[k * TB : (k + 1) * TB]

            @pl.when(jnp.logical_not(own))
            def _():
                owner_copy(f, d, k).start()

    def combine(f, j):
        combine_one(f, (z + NZ - j) % NZ)

        @pl.when((j > 0) & (j < 4))
        def _():
            combine_one(f, (z + j) % NZ)

    def hpair(b, j):
        return jnp.concatenate([H[b, (z + NZ - j) % NZ], H[b, (z + j) % NZ]], axis=0)

    def stage(f, j, wide, low, width):
        for n, d in enumerate(((z + NZ - j) % NZ, (z + j) % NZ)):
            ST[f, d, :, 0:D] = wide[n * CH : (n + 1) * CH].astype(BF16)
            ST[f, d, :, D : D + width] = low[n * CH : (n + 1) * CH].astype(BF16)

    ST[0, :, :, D + R : W] = jnp.zeros((NZ, CH, R), BF16)

    @pl.loop(0, 5)
    def _(j):
        chain_wait(0, j)

        @pl.when((j > 0) & (j < 4))
        def _():
            chain_start(0, j + 1)

        x = hpair(0, j)
        stage(0, j, nn(x, VD[...]), nn(x, AD[...]), R)
        sib_start(0, j)

        @pl.when(j > 0)
        def _():
            combine(1, j - 1)

        chain_wait(1, j)

        @pl.when((j > 0) & (j < 4))
        def _():
            chain_start(1, j + 1)

        chain_wait(2, j)

        @pl.when((j > 0) & (j < 4))
        def _():
            chain_start(2, j + 1)

        xg, xu = hpair(1, j), hpair(2, j)
        low = jnp.where(
            lax.broadcasted_iota(jnp.int32, (2 * CH, 128), 1) < R, nt(xg, BGU[...]), nt(xu, BGU[...])
        )
        stage(1, j, nt(xg, VG[...]) + nt(xu, VU[...]), low, 128)
        sib_start(1, j)
        combine(0, j)

    combine(1, 4)

    def rows_total(f):
        @pl.loop(0, NC)
        def _(s):
            @pl.when(s != q)
            def _():
                remote(RX.at[f, s], RX.at[f, s], rxs.at[f, 0], rxr.at[f, s], z, g).wait_recv()

        return jnp.sum(RX[f].astype(F32), axis=0)

    total = rows_total(0)
    down_low = total[:, D : D + R].astype(BF16)
    DL[me, :, 0:R] = down_low

    @pl.loop(1, NG)
    def _(k):
        remote(DL.at[me], DL.at[me], dls.at[k], dlr.at[k], z, (g + k) % NG).start()

    out[...] = (total[:, 0:D] + SCALE * nn(down_low, BD[...])).astype(BF16)

    for b, ref in ((1, gmap), (2, umap)):
        low = LA[:, (b - 1) * TB : b * TB, :].reshape(NG * TB, 128)
        LOWF[...] = SCALE * tn(low, H[b].reshape(NG * TB, FF))
        ref[...] = LOWF[pl.ds(pl.multiple_of(8 * z, 8), 8)]

    total = rows_total(1)
    back = total[:, D:W].astype(BF16)
    tig[...] = (
        total[:, 0:D] + SCALE * (nt(back[:, 0:R], AG[...]) + nt(pltpu.roll(back.astype(F32), R, 1).astype(BF16)[:, 0:R], AU[...]))
    ).astype(BF16)

    @pl.loop(1, NG)
    def _(k):
        p = (g + NG - k) % NG
        s = slot_of(p // 2, p % 2)
        remote(DL.at[s], DL.at[s], dls.at[k], dlr.at[k], z, g).wait_recv()

    grads = SCALE * tn(DL[...].reshape(NG * TB, 128), X[1].reshape(NG * TB, D))
    rank = lax.broadcasted_iota(jnp.int32, (128, D), 0)
    for k in range(2):
        dmap[k : k + 1] = jnp.sum(jnp.where(rank == 2 * g + k, grads, 0.0), axis=0, keepdims=True)

    @pl.loop(1, NC)
    def _(k):
        for a in range(2):
            remote(X.at[a, me], X.at[a, me], xs.at[a, k], xr.at[a, k], z, g).wait_send()

    @pl.loop(0, NC)
    def _(k):
        for a in range(2):
            remote(X.at[a, me], X.at[a, me], ys.at[a, k], yr.at[a, k], z, g).wait_send()

    @pl.loop(1, NZ)
    def _(k):
        remote(LZ.at[z], LZ.at[z], lzs.at[k], lzr.at[k], z, g).wait_send()

    @pl.loop(1, NG)
    def _(k):
        remote(LA.at[me], LA.at[me], las.at[k], lar.at[k], z, g).wait_send()
        remote(DL.at[me], DL.at[me], dls.at[k], dlr.at[k], z, g).wait_send()

    for a in range(3):
        for way in range(2):
            ring_copy(a, way, 4, True).wait_send()
            chain_copy(a, way, 4, True, False).wait_send()

            @pl.loop(1, 4)
            def _(j):
                ring_copy(a, way, j, False).wait_send()
                chain_copy(a, way, j, False, False).wait_send()

    @pl.loop(0, NZ)
    def _(d):
        for f in range(2):
            sib_copy(f, d).wait_send()
            for k in range(2):
                @pl.when(owner_chip(d, k) != q)
                def _():
                    owner_copy(f, d, k).wait_send()


def body(*args):
    dma = pltpu.SemaphoreType.DMA
    hbm = pl.BlockSpec(memory_space=pl.ANY)
    vmem = pl.BlockSpec(memory_space=pltpu.VMEM)
    return pl.pallas_call(
        kernel,
        out_shape=(
            jax.ShapeDtypeStruct((TB, D), BF16),
            jax.ShapeDtypeStruct((TB, D), BF16),
            jax.ShapeDtypeStruct((8, FF), F32),
            jax.ShapeDtypeStruct((8, FF), F32),
            jax.ShapeDtypeStruct((2, D), F32),
        ),
        in_specs=[hbm] * 11,
        out_specs=(vmem,) * 5,
        scratch_shapes=[
            pltpu.VMEM((2, NG, TB, D), BF16),
            pltpu.VMEM((D, FF), BF16),
            pltpu.VMEM((D, FF), BF16),
            pltpu.VMEM((FF, D), BF16),
            pltpu.VMEM((D, R), BF16),
            pltpu.VMEM((D, R), BF16),
            pltpu.VMEM((FF, R), BF16),
            pltpu.VMEM((2 * R, FF), BF16),
            pltpu.VMEM((R, D), BF16),
            pltpu.VMEM((NZ, 3 * TB, 128), BF16),
            pltpu.VMEM((NG, 3 * TB, 128), BF16),
            pltpu.VMEM((NG, TB, 128), BF16),
            pltpu.VMEM((2 * CH, FF), F32),
            pltpu.VMEM((2 * CH, FF), F32),
            pltpu.VMEM((2 * CH, FF), F32),
            pltpu.VMEM((CH, FF), F32),
            pltpu.VMEM((CH, FF), F32),
            pltpu.VMEM((3, 2, 4, CH, FF), BF16),
            pltpu.VMEM((3, 2, 5, CH, FF), BF16),
            pltpu.VMEM((3, NZ, CH, FF), BF16),
            pltpu.VMEM((2, NZ, CH, W), BF16),
            pltpu.VMEM((2, NZ, CH // 2, W), BF16),
            pltpu.VMEM((2, NZ, CH // 2, W), BF16),
            pltpu.VMEM((2, NC, TB, W), BF16),
            pltpu.VMEM((128, FF), F32),
            dma((9,)),
            dma((2,)),
            dma((2, NC)),
            dma((2, NC)),
            dma((2, NC)),
            dma((2, NC)),
            dma((NZ,)),
            dma((NZ,)),
            dma((NG,)),
            dma((NG,)),
            dma((NG,)),
            dma((NG,)),
            dma((3, 2, 4)),
            dma((3, 2, 4)),
            dma((3, 2, 4)),
            dma((3, 2, 4)),
            dma((2, NZ)),
            dma((2, NZ)),
            dma((2, 2 * NZ)),
            dma((2, NC)),
        ],
        compiler_params=pltpu.CompilerParams(
            collective_id=0, has_side_effects=True, vmem_limit_bytes=48 * 1024 * 1024
        ),
    )(*args)


def solution(mesh):
    in_specs = (
        P("gy", "gx"),
        P("gx", "gy"),
        P("gx", "gy"),
        P("gy", "gx"),
        P("gx", None),
        P("gx", None),
        P("gy", None),
        P(None, "gy"),
        P(None, "gy"),
        P(None, "gx"),
        P("gy", "gx"),
    )
    out_specs = (P("gy", "gx"), P("gy", "gx"), P("gx", "gy"), P("gx", "gy"), P("gy", "gx"))
    return jax.shard_map(body, mesh=mesh, in_specs=in_specs, out_specs=out_specs, check_vma=False)
```

time: 945 us -> 119 us (0.13)
  waiting for transfers between devices: 817 us -> 0 us
  Pallas kernels: 0 us -> 104 us
  blocking collectives: 64.8 us -> 0 us
  matrix products: 37.2 us -> 0 us
  between operations: 15.3 us -> 0.68 us
    reduce_scatter x7 -> x0, waiting for transfers between devices: 440 us -> none  [the longest x1 99.8 us: body(): lax.psum_scatter(down_terms, 'gy', scatter_dimension=0, tiled=True)]
    unnamed x17 -> x0, waiting for transfers between devices: 284 us -> none
    pallas_call x0 -> x1, Pallas kernels: none -> 104 us  [body(): pl.pallas_call(kernel, out_shape=(jax.ShapeDtypeStruct((TB, D), BF16), ja...]
    all_gather x2 -> x0, waiting for transfers between devices: 92.7 us -> none  [the longest x1 53.9 us: body(): rows_all = lax.all_gather(tokens, 'gy', axis=0, tiled=True)]
    all_gather x3 -> x0, blocking collectives: 64.8 us -> none  [the longest x1 22.8 us: body(): lax.all_gather(upward_gradient, 'gx', axis=0, tiled=True)]
    dot_general x20 -> x0, matrix products: 37.2 us -> none  [the longest x8 17.5 us: gated_product(): return jnp.dot(left, right, preferred_element_type=jnp.float32)]
  transfers between devices with their start and end apart: 13 -> 0, of which waited for: 13 -> 0; matrix products, arithmetic and copies ran while one was open for 4% -> 0% of each run, Pallas kernels for 0% -> 0%
where the time goes in v1:
time: 119 us; the launch traced here: 118 us
  Pallas kernels  104 us (87%)
  local copies, waits for them, and re-layouts  13.5 us (11%)
    pallas_call x1, Pallas kernels, body(): pl.pallas_call(kernel, out_shape=(jax.ShapeDtypeStruct((TB, D), BF16), ja...  104 us
    unnamed x22, local copies, waits for them, and re-layouts  13.5 us

profile of v1, /device:TPU:1, one launch (start us, length us, event | category | flops | bytes accessed | tf_op | source)
XLA Modules:
  0.0 118.2 jit_solution(3833905003089258184)
XLA Ops:
  0.6 1.1 copy.18.ad
  1.7 1.1 copy.16.ag
  2.8 1.1 copy.17.au
  3.9 0.0 copy-start
  3.9 1.5 %copy-done = bf16[1024,896]{1,0:T(8,128)(2,1)S(1)} copy-done((bf16[1024,896]{1,0:T(8,128)(2,1)S(1)}, bf16[1024,896]{1,0:T(8,128)(2,1)}, u32[]{:S(2)}) %copy-start) | copy-done | bytes 1835032
  5.4 0.0 copy-start.1
  5.4 1.5 %copy-done.1 = bf16[1024,896]{1,0:T(8,128)(2,1)S(1)} copy-done((bf16[1024,896]{1,0:T(8,128)(2,1)S(1)}, bf16[1024,896]{1,0:T(8,128)(2,1)}, u32[]{:S(2)}) %copy-start.1) | copy-done | bytes 1835032
  6.9 0.0 copy-start.2
  6.9 0.9 copy-done.2
  7.8 0.0 copy-start.3
  7.8 0.9 copy-done.3
  8.7 0.0 copy-start.4
  8.7 0.9 copy-done.4
  9.6 0.0 copy-start.5
  9.6 0.8 copy-done.5
  10.3 0.0 copy-start.6
  10.3 0.8 copy-done.6
  11.1 104.1 %shard_map.146 = (bf16[16,1024]{1,0:T(8,128)(2,1)S(1)}, bf16[16,1024]{1,0:T(8,128)(2,1)S(1)}, f32[8,896]{1,0:T(8,128)S(1)}, f32[8,896]{1,0:T(8,128)S(1)}, f32[2,1024]{1,0:T(2,128)S(1)}) custom-call(bf16[16,1024]{1,0:T(8,128)(2,1)S(1)} %copy-done.5, bf16[1024,896]{1,0:T(8,128)(2,1)S(1)} %copy-done, bf16[1024,896]{1,0:T(8,128)(2,1)S(1)} %copy-done.1, ...), custom_call_target="tpu_custom_call" | custom-call | tf_op jit(solution)/shard_map/pallas_call | solution.py:461
  115.2 0.6 copy.24
  115.8 0.6 copy.25
  116.4 0.6 copy.26
  117.0 0.6 copy.27
  117.6 0.6 copy.28
Async XLA Ops:
  3.9 1.5 %copy-start = (bf16[1024,896]{1,0:T(8,128)(2,1)S(1)}, bf16[1024,896]{1,0:T(8,128)(2,1)}, u32[]{:S(2)}) copy-start(bf16[1024,896]{1,0:T(8,128)(2,1)} %wg.1) | copy-start | bytes 5505028
  5.4 1.5 %copy-start.1 = (bf16[1024,896]{1,0:T(8,128)(2,1)S(1)}, bf16[1024,896]{1,0:T(8,128)(2,1)}, u32[]{:S(2)}) copy-start(bf16[1024,896]{1,0:T(8,128)(2,1)} %wu.1) | copy-start | bytes 5505028
  6.9 0.9 copy-start.2
  7.8 0.9 copy-start.3
  8.7 0.9 copy-start.4
  9.6 0.8 copy-start.5
  10.3 0.8 copy-start.6

commit v2 on v1

v2 whole, which is shorter than its diff:
```python
import functools

import jax
import jax.numpy as jnp
from jax import lax
from jax.experimental import pallas as pl
from jax.experimental.pallas import tpu as pltpu
from jax.sharding import PartitionSpec as P

MESH = pl.DeviceIdType.MESH
F32 = jnp.float32
BF16 = jnp.bfloat16

NZ = 8
NG = 32
SIDE = 4
NC = 16
TB = 16
CH = 64
D = 1024
FF = 896
R = 64
W = D + 128
SCALE = 0.5
VMEM = 60 * 1024 * 1024


def mod(a, m):
    return lax.rem(a, m)


def nn(left, right):
    return jnp.dot(left, right, preferred_element_type=F32)


def nt(left, right):
    return lax.dot_general(left, right, (((1,), (1,)), ((), ())), preferred_element_type=F32)


def tn(left, right):
    return lax.dot_general(left, right, (((0,), (0,)), ((), ())), preferred_element_type=F32)


def kernel(
    tok, wg, wu, wd, ag, au, ad, bg, bu, bd, cot,
    out, tig, gmap, umap, dmap,
    X, VG, VU, VD, AGU, AD, BGU, BD,
    LZ, LA, DL, PG, PU, PH, WIDE, GA, UA, RS, RR, H, ST, SB, O2, RX, LOWF,
    wsem, xsem, xs, xr, vs, vr, ys, yr, lzs, lzr, las, lar, dls, dlr, rss, rsr, ags, agr, sbs, sbr, rxs, rxr,
):
    z = lax.axis_index("gx")
    g = lax.axis_index("gy")
    q, c = lax.div(g, 2), mod(g, 2)
    qx, qy = mod(q, SIDE), lax.div(q, SIDE)
    sibling = g + 1 - 2 * c
    right, left = mod(z + 1, NZ), mod(z + NZ - 1, NZ)

    columns = [2 * mod(qx + i, SIDE) for i in range(SIDE)]
    rows = [8 * mod(qy + i, SIDE) for i in range(SIDE)]
    first = [a + c * (b - a) for a, b in zip(columns, rows)]
    second = [b + c * (a - b) for a, b in zip(columns, rows)]

    def device_at(i, k):
        return first[i % SIDE] + second[k % SIDE] + c

    def sibling_at(i, k):
        return second[i % SIDE] + first[k % SIDE] + 1 - c

    def owner(d, cc, k):
        return 4 * mod(d + 4 * cc, NZ) + 2 * k + cc

    def owners(d):
        return [owner(d, p // 2, p % 2) for p in range(4)]

    def remote(src, dst, ssem, rsem, zz, gg):
        return pltpu.make_async_remote_copy(
            src_ref=src, dst_ref=dst, send_sem=ssem, recv_sem=rsem, device_id=(zz, gg), device_id_type=MESH
        )

    me = g

    own_copies = [
        pltpu.make_async_copy(tok, X.at[0, me], xsem.at[0]),
        pltpu.make_async_copy(cot, X.at[1, me], xsem.at[1]),
    ]
    low_copies = [
        pltpu.make_async_copy(ag, AGU.at[pl.ds(0, R)], wsem.at[0]),
        pltpu.make_async_copy(au, AGU.at[pl.ds(R, R)], wsem.at[1]),
        pltpu.make_async_copy(bd, BD, wsem.at[2]),
    ]
    gate_copies = [
        pltpu.make_async_copy(wg, VG, wsem.at[3]),
        pltpu.make_async_copy(wu, VU, wsem.at[4]),
    ]
    rest_copies = [
        pltpu.make_async_copy(wd, VD, wsem.at[5]),
        pltpu.make_async_copy(ad, AD, wsem.at[6]),
        pltpu.make_async_copy(bg, BGU.at[pl.ds(0, R)], wsem.at[7]),
        pltpu.make_async_copy(bu, BGU.at[pl.ds(R, R)], wsem.at[8]),
    ]
    for copy in own_copies + low_copies + gate_copies + rest_copies:
        copy.start()

    barrier = pltpu.get_barrier_semaphore()

    @pl.loop(1, NG)
    def _(k):
        pl.semaphore_signal(barrier, inc=1, device_id=(z, mod(g + k, NG)), device_id_type=MESH)

    @pl.loop(1, NZ)
    def _(k):
        pl.semaphore_signal(barrier, inc=1, device_id=(mod(z + k, NZ), g), device_id_type=MESH)

    zero_half = jnp.zeros((3, CH // 2, FF), BF16)
    RR[:, 0, 3, CH // 2 : CH, :] = zero_half
    RR[:, 1, 3, 0 : CH // 2, :] = zero_half
    RR[:, :, 4] = jnp.zeros((3, 2, CH, FF), BF16)
    LZ[z] = jnp.zeros((2 * TB, 128), BF16)
    DL[me] = jnp.zeros((TB, 128), BF16)

    for copy in own_copies:
        copy.wait()

    for copy in low_copies:
        copy.wait()
    LZ[z, 0:TB] = nt(X[0, me], AGU[...]).astype(BF16)
    LZ[z, TB : 2 * TB, 0:R] = nt(X[1, me], BD[...]).astype(BF16)


    pl.semaphore_wait(barrier, NG - 1 + NZ - 1)

    def near(a, s, i):
        return remote(X.at[a, s], X.at[a, s], xs.at[a, i], xr.at[a, i], z, device_at(i, 0))

    def far(a, s, i, k):
        return remote(X.at[a, s], X.at[a, s], vs.at[a, i, k], vr.at[a, i, k], z, device_at(0, k))

    def relay(a, s, i, k):
        return remote(X.at[a, s], X.at[a, s], ys.at[a, i, k], yr.at[a, i, k], z, sibling)

    def spread_near(a):
        for i in (1, 3, 2):
            near(a, me, i).start()
        relay(a, me, 0, 0).start()

    def spread_turn(a):
        for k in (1, 3, 2):
            far(a, me, 0, k).start()
        for i in (1, 3, 2):
            s = device_at(-i, 0)
            near(a, s, i).wait_recv()
            for k in (1, 3, 2):
                far(a, s, i, k).start()
            relay(a, s, i, 0).start()

    def spread_far(a):
        for k in (3, 1, 2):
            for i in (0, 1, 3, 2):
                s = device_at(-i, -k)
                far(a, s, i, k).wait_recv()
                relay(a, s, i, k).start()

    def spread_wait(a):
        for k in (0, 3, 1, 2):
            for i in (0, 1, 3, 2):
                relay(a, sibling_at(-i, -k), i, k).wait_recv()

    spread_near(0)
    spread_near(1)
    @pl.loop(1, NZ)
    def _(k):
        remote(LZ.at[z], LZ.at[z], lzs.at[k], lzr.at[k], mod(z + k, NZ), g).start()

    spread_turn(0)
    spread_turn(1)
    spread_far(0)
    spread_wait(0)

    def to_plane(ref, ssem, rsem, k):
        return remote(ref.at[me], ref.at[me], ssem.at[k], rsem.at[k], z, mod(g + k, NG))

    def from_plane(ref, ssem, rsem, k):
        s = mod(g + NG - k, NG)
        return remote(ref.at[s], ref.at[s], ssem.at[k], rsem.at[k], z, g)

    def low_sum():
        @pl.loop(1, NZ)
        def _(k):
            s = mod(z + NZ - k, NZ)
            remote(LZ.at[s], LZ.at[s], lzs.at[k], lzr.at[k], z, g).wait_recv()

        LA[me] = jnp.sum(LZ[...].astype(F32), axis=0).astype(BF16)

        @pl.loop(1, NG)
        def _(k):
            to_plane(LA, las, lar, k).start()

    def low_wait():
        @pl.loop(1, NG)
        def _(k):
            from_plane(LA, las, lar, k).wait_recv()

    for copy in gate_copies + rest_copies:
        copy.wait()

    def ring_copy(a, way, j, half):
        rows = pl.ds(way * (CH // 2), CH // 2) if half else pl.ds(0, CH)
        return remote(
            RS.at[a, way, j - 1, rows], RR.at[a, way, j - 1, rows],
            rss.at[a, way, j - 1], rsr.at[a, way, j - 1], left if way else right, g,
        )

    def ring_wait(a, j):
        @pl.when(j == 3)
        def _():
            ring_copy(a, 0, 4, True).wait_recv()
            ring_copy(a, 1, 4, True).wait_recv()

        @pl.when(j < 3)
        def _():
            ring_copy(a, 0, j + 1, False).wait_recv()
            ring_copy(a, 1, j + 1, False).wait_recv()

    def pair(a, j):
        return jnp.concatenate([X[a, p] for d in (mod(z + j, NZ), mod(z + NZ - j, NZ)) for p in owners(d)], axis=0)

    def ring_step(a, part, j):
        ring_wait(a, j)

        @pl.when(j > 0)
        def _():
            RS[a, 0, j - 1] = (part[0:CH] + RR[a, 0, j].astype(F32)).astype(BF16)
            RS[a, 1, j - 1] = (part[CH : 2 * CH] + RR[a, 1, j].astype(F32)).astype(BF16)

        @pl.when(j == 4)
        def _():
            ring_copy(a, 0, 4, True).start()
            ring_copy(a, 1, 4, True).start()

        @pl.when((j > 0) & (j < 4))
        def _():
            ring_copy(a, 0, j, False).start()
            ring_copy(a, 1, j, False).start()

    def ring_total(a, part):
        return part[0:CH] + (RR[a, 0, 0].astype(F32) + RR[a, 1, 0].astype(F32))

    def low_chunk(which):
        return jnp.concatenate([LA[p, which * TB : (which + 1) * TB] for p in owners(z)], axis=0)

    def half_rows(low, first):
        lane = lax.broadcasted_iota(jnp.int32, low.shape, 1)
        return jnp.where((lane < R) == first, low, jnp.zeros_like(low))

    def chain_copy(b, way, j, half, arriving):
        hops = j if arriving else j - 1
        d = mod(z + hops, NZ) if way else mod(z + NZ - hops, NZ)
        rows = pl.ds(way * (CH // 2), CH // 2) if half else pl.ds(0, CH)
        return remote(
            H.at[b, d, rows], H.at[b, d, rows],
            ags.at[b, way, j - 1], agr.at[b, way, j - 1], left if way else right, g,
        )

    def chain_start(b, j):
        @pl.when(j == 4)
        def _():
            chain_copy(b, 0, 4, True, False).start()
            chain_copy(b, 1, 4, True, False).start()

        @pl.when(j < 4)
        def _():
            chain_copy(b, 0, j, False, False).start()
            chain_copy(b, 1, j, False, False).start()

    def chain_wait(b, j):
        @pl.when(j == 4)
        def _():
            chain_copy(b, 0, 4, True, True).wait_recv()
            chain_copy(b, 1, 4, True, True).wait_recv()

        @pl.when((j > 0) & (j < 4))
        def _():
            chain_copy(b, 0, j, False, True).wait_recv()
            chain_copy(b, 1, j, False, True).wait_recv()

    @pl.loop(0, 6)
    def _(i):
        @pl.when(i < 5)
        def _():
            j = 4 - i
            x = pair(0, j)
            PG[...] = nn(x, VG[...])
            ring_step(0, PG, j)
            PU[...] = nn(x, VU[...])
            ring_step(1, PU, j)

            @pl.when(j == 0)
            def _():
                low_wait()
                low = low_chunk(0)
                gate = ring_total(0, PG) + SCALE * nn(half_rows(low, True), BGU[...])
                up = ring_total(1, PU) + SCALE * nn(half_rows(low, False), BGU[...])
                GA[...] = gate
                UA[...] = up
                H[0, z] = (gate * jax.nn.sigmoid(gate) * up).astype(BF16)
                chain_start(0, 1)

        @pl.when(i == 0)
        def _():
            spread_far(1)

        @pl.when(i == 1)
        def _():
            spread_wait(1)

        @pl.when(i == 5)
        def _():
            chain_wait(0, 1)
            chain_start(0, 2)

        @pl.when(i > 0)
        def _():
            j = 5 - i
            PH[...] = nt(pair(1, j), VD[...])
            ring_step(2, PH, j)

            @pl.when(j == 0)
            def _():
                grad = ring_total(2, PH) + SCALE * nn(low_chunk(1)[:, 0:R], AD[...])
                gate, up = GA[...], UA[...]
                sigma = jax.nn.sigmoid(gate)
                H[1, z] = (grad * up * sigma * (1.0 + gate * (1.0 - sigma))).astype(BF16)
                chain_start(1, 1)
                H[2, z] = (grad * gate * sigma).astype(BF16)
                chain_start(2, 1)

        @pl.when(i == 1)
        def _():
            low_sum()

    def sib_copy(f, d):
        rows = pl.ds(pl.multiple_of((1 - c) * 32, 32), 32)
        return remote(ST.at[f, d, rows], SB.at[f, d], sbs.at[f, d], sbr.at[f, d], z, sibling)

    def sib_start(f, j):
        da, db = mod(z + NZ - j, NZ), mod(z + j, NZ)
        sib_copy(f, da).start()

        @pl.when((j > 0) & (j < 4))
        def _():
            sib_copy(f, db).start()

    def owner_copy(f, d, k):
        return remote(
            O2.at[f, d, pl.ds(k * TB, TB)], RX.at[f, q], rxs.at[f, 2 * d + k], rxr.at[f, q],
            z, owner(d, c, k),
        )

    def combine_one(f, d):
        sib_copy(f, d).wait_recv()
        rows = pl.ds(pl.multiple_of(c * 32, 32), 32)
        total = (ST[f, d, rows].astype(F32) + SB[f, d].astype(F32)).astype(BF16)
        O2[f, d] = total
        for k in range(2):
            own = owner(d, c, k) == g

            @pl.when(own)
            def _():
                RX[f, q] = total[k * TB : (k + 1) * TB]

            @pl.when(jnp.logical_not(own))
            def _():
                owner_copy(f, d, k).start()

    def combine(f, j):
        combine_one(f, mod(z + NZ - j, NZ))

        @pl.when((j > 0) & (j < 4))
        def _():
            combine_one(f, mod(z + j, NZ))

    def hpair(b, j):
        return jnp.concatenate([H[b, mod(z + NZ - j, NZ)], H[b, mod(z + j, NZ)]], axis=0)

    def adapter_grads(b, j, x):
        low = jnp.concatenate([LA[p, 0:TB] for d in (mod(z + NZ - j, NZ), mod(z + j, NZ)) for p in owners(d)], axis=0)
        once = (lax.broadcasted_iota(jnp.int32, (2 * CH, 128), 0) < CH) | (mod(j, 4) > 0)
        LOWF[b] += tn(jnp.where(once, low, jnp.zeros_like(low)), x)

    LOWF[...] = jnp.zeros((2, 128, FF), F32)

    def stage(f, j, wide, low, width):
        for n, d in enumerate((mod(z + NZ - j, NZ), mod(z + j, NZ))):
            ST[f, d, :, 0:D] = wide[n * CH : (n + 1) * CH].astype(BF16)
            ST[f, d, :, D : D + width] = low[n * CH : (n + 1) * CH].astype(BF16)

    ST[0, :, :, D + R : W] = jnp.zeros((NZ, CH, R), BF16)

    def rows_total(f):
        @pl.loop(0, NC)
        def _(s):
            @pl.when(s != q)
            def _():
                remote(RX.at[f, s], RX.at[f, s], rxs.at[f, 0], rxr.at[f, s], z, g).wait_recv()

        return jnp.sum(RX[f].astype(F32), axis=0)

    def chain_pass(b, j):
        @pl.when(j > 0)
        def _():
            chain_wait(b, j)

            @pl.when(j < 4)
            def _():
                chain_start(b, j + 1)

    @pl.loop(0, 6)
    def _(u):
        j = u - 1

        @pl.when((u > 1) & (u < 5))
        def _():
            chain_pass(0, u)

        @pl.when(u < 5)
        def _():
            x = hpair(0, u)
            stage(0, u, nn(x, VD[...]), nt(x, AD[...]), R)
            sib_start(0, u)

        @pl.when(j > 0)
        def _():
            combine(1, j - 1)

        @pl.when(j >= 0)
        def _():
            chain_pass(1, j)
            x = hpair(1, j)
            WIDE[:, 0:D] = nt(x, VG[...])
            WIDE[:, D:W] = nt(x, BGU[...])
            adapter_grads(0, j, x)

        @pl.when(u < 5)
        def _():
            combine(0, u)

        @pl.when(u == 5)
        def _():
            total = rows_total(0)
            down_low = total[:, D : D + R].astype(BF16)
            DL[me, :, 0:R] = down_low

            @pl.loop(1, NG)
            def _(k):
                to_plane(DL, dls, dlr, k).start()

            out[...] = (total[:, 0:D] + SCALE * nn(down_low, BD[...])).astype(BF16)

        @pl.when(j >= 0)
        def _():
            chain_pass(2, j)
            x = hpair(2, j)
            lane = lax.broadcasted_iota(jnp.int32, (2 * CH, 128), 1)
            low = jnp.where(lane < R, WIDE[:, D:W], nt(x, BGU[...]))
            stage(1, j, WIDE[:, 0:D] + nt(x, VU[...]), low, 128)
            sib_start(1, j)
            adapter_grads(1, j, x)

    for b, ref in ((0, gmap), (1, umap)):
        ref[...] = SCALE * LOWF[b, pl.ds(pl.multiple_of(R * b + 8 * z, 8), 8)]

    combine(1, 4)

    for a in range(2):
        for i in range(SIDE):
            for k in range(SIDE):
                if k:
                    far(a, me, i, k).wait_send()
                elif i:
                    near(a, me, i).wait_send()
                relay(a, me, i, k).wait_send()

    @pl.loop(1, NZ)
    def _(k):
        remote(LZ.at[z], LZ.at[z], lzs.at[k], lzr.at[k], z, g).wait_send()

    @pl.loop(1, NG)
    def _(k):
        to_plane(LA, las, lar, k).wait_send()

    for a in range(3):
        for way in range(2):
            ring_copy(a, way, 4, True).wait_send()

            @pl.loop(1, 4)
            def _(j):
                ring_copy(a, way, j, False).wait_send()

    @pl.loop(1, NG)
    def _(k):
        from_plane(DL, dls, dlr, k).wait_recv()

    grads = SCALE * tn(DL[...].reshape(NG * TB, 128), X[1].reshape(NG * TB, D))
    rank = lax.broadcasted_iota(jnp.int32, (128, D), 0)
    for k in range(2):
        dmap[k : k + 1] = jnp.sum(jnp.where(rank == 2 * g + k, grads, 0.0), axis=0, keepdims=True)

    total = rows_total(1)
    back = total[:, D:W].astype(BF16)
    tig[...] = (total[:, 0:D] + SCALE * nn(back, AGU[...])).astype(BF16)

    @pl.loop(1, NG)
    def _(k):
        to_plane(DL, dls, dlr, k).wait_send()

    for a in range(3):
        for way in range(2):
            chain_copy(a, way, 4, True, False).wait_send()

            @pl.loop(1, 4)
            def _(j):
                chain_copy(a, way, j, False, False).wait_send()

    @pl.loop(0, NZ)
    def _(d):
        for f in range(2):
            sib_copy(f, d).wait_send()
            for k in range(2):
                @pl.when(owner(d, c, k) != g)
                def _():
                    owner_copy(f, d, k).wait_send()


def place(*refs):
    for a, b in zip(refs[:5], refs[5:]):
        b[...] = a[...]


def body(tok, wg, wu, wd, ag, au, ad, bg, bu, bd, cot):
    dma = pltpu.SemaphoreType.DMA
    hbm = pl.BlockSpec(memory_space=pltpu.HBM)
    vmem = pl.BlockSpec(memory_space=pltpu.VMEM)
    args = (tok, wg, wu, wd, ag.T, au.T, ad.T, bg, bu, bd, cot)
    results = pl.pallas_call(
        kernel,
        out_shape=(
            jax.ShapeDtypeStruct((TB, D), BF16),
            jax.ShapeDtypeStruct((TB, D), BF16),
            jax.ShapeDtypeStruct((8, FF), F32),
            jax.ShapeDtypeStruct((8, FF), F32),
            jax.ShapeDtypeStruct((2, D), F32),
        ),
        in_specs=[hbm] * 11,
        out_specs=(vmem,) * 5,
        scratch_shapes=[
            pltpu.VMEM((2, NG, TB, D), BF16),
            pltpu.VMEM((D, FF), BF16),
            pltpu.VMEM((D, FF), BF16),
            pltpu.VMEM((FF, D), BF16),
            pltpu.VMEM((2 * R, D), BF16),
            pltpu.VMEM((R, FF), BF16),
            pltpu.VMEM((2 * R, FF), BF16),
            pltpu.VMEM((R, D), BF16),
            pltpu.VMEM((NZ, 2 * TB, 128), BF16),
            pltpu.VMEM((NG, 2 * TB, 128), BF16),
            pltpu.VMEM((NG, TB, 128), BF16),
            pltpu.VMEM((2 * CH, FF), F32),
            pltpu.VMEM((2 * CH, FF), F32),
            pltpu.VMEM((2 * CH, FF), F32),
            pltpu.VMEM((2 * CH, W), F32),
            pltpu.VMEM((CH, FF), F32),
            pltpu.VMEM((CH, FF), F32),
            pltpu.VMEM((3, 2, 4, CH, FF), BF16),
            pltpu.VMEM((3, 2, 5, CH, FF), BF16),
            pltpu.VMEM((3, NZ, CH, FF), BF16),
            pltpu.VMEM((2, NZ, CH, W), BF16),
            pltpu.VMEM((2, NZ, CH // 2, W), BF16),
            pltpu.VMEM((2, NZ, CH // 2, W), BF16),
            pltpu.VMEM((2, NC, TB, W), BF16),
            pltpu.VMEM((2, 128, FF), F32),
            dma((9,)),
            dma((2,)),
            dma((2, SIDE)),
            dma((2, SIDE)),
            dma((2, SIDE, SIDE)),
            dma((2, SIDE, SIDE)),
            dma((2, SIDE, SIDE)),
            dma((2, SIDE, SIDE)),
            dma((NZ,)),
            dma((NZ,)),
            dma((NG,)),
            dma((NG,)),
            dma((NG,)),
            dma((NG,)),
            dma((3, 2, 4)),
            dma((3, 2, 4)),
            dma((3, 2, 4)),
            dma((3, 2, 4)),
            dma((2, NZ)),
            dma((2, NZ)),
            dma((2, 2 * NZ)),
            dma((2, NC)),
        ],
        compiler_params=pltpu.CompilerParams(
            collective_id=0, has_side_effects=True, vmem_limit_bytes=VMEM
        ),
    )(*args)
    return pl.pallas_call(
        place,
        out_shape=tuple(jax.ShapeDtypeStruct(r.shape, r.dtype) for r in results),
        in_specs=[vmem] * 5,
        out_specs=(vmem,) * 5,
    )(*results)


def solution(mesh):
    in_specs = (
        P("gy", "gx"),
        P("gx", "gy"),
        P("gx", "gy"),
        P("gy", "gx"),
        P("gx", None),
        P("gx", None),
        P("gy", None),
        P(None, "gy"),
        P(None, "gy"),
        P(None, "gx"),
        P("gy", "gx"),
    )
    out_specs = (P("gy", "gx"), P("gy", "gx"), P("gx", "gy"), P("gx", "gy"), P("gy", "gx"))
    return jax.shard_map(body, mesh=mesh, in_specs=in_specs, out_specs=out_specs, check_vma=False)
```

time: 119 us -> 94.9 us (0.80)
  local copies, waits for them, and re-layouts: 13.5 us -> 0 us
  Pallas kernels: 104 us -> 94.1 us
    unnamed x22 -> x0, local copies, waits for them, and re-layouts: 13.5 us -> none
    pallas_call x1, Pallas kernels: 104 us -> 92.7 us  [body(): pl.pallas_call(kernel, out_shape=(jax.ShapeDtypeStruct((TB, D), BF16), ja...]
    pallas_call x0 -> x1, Pallas kernels: none -> 1.45 us  [body(): pl.pallas_call(place, out_shape=tuple((jax.ShapeDtypeStruct(r.shape, r.dt...]
where the time goes in v2:
time: 94.9 us; the launch traced here: 94.8 us
  Pallas kernels  94.1 us (99%)
    pallas_call x1, Pallas kernels, body(): pl.pallas_call(kernel, out_shape=(jax.ShapeDtypeStruct((TB, D), BF16), ja...  92.7 us

profile of v2, /device:TPU:1, one launch (start us, length us, event | category | flops | bytes accessed | tf_op | source)
XLA Modules:
  0.0 94.8 jit_solution(4176318329533734924)
XLA Ops:
  0.6 92.7 %shard_map.146 = (bf16[16,1024]{1,0:T(8,128)(2,1)}, bf16[16,1024]{1,0:T(8,128)(2,1)}, f32[8,896]{1,0:T(8,128)}, f32[8,896]{1,0:T(8,128)}, f32[2,1024]{1,0:T(2,128)}) custom-call(bf16[16,1024]{1,0:T(8,128)(2,1)} %tok.1, bf16[1024,896]{1,0:T(8,128)(2,1)} %wg.1, bf16[1024,896]{1,0:T(8,128)(2,1)} %wu.1, bf16[896,1024]{1,0:T(8,128)(2,1)} %wd.1, ...), custom_call_target="tpu_custom_call" | custom-call | tf_op jit(solution)/shard_map/pallas_call | solution.py:544
  93.3 1.4 %shard_map.147 = (bf16[16,1024]{1,0:T(8,128)(2,1)}, bf16[16,1024]{1,0:T(8,128)(2,1)}, f32[8,896]{1,0:T(8,128)}, f32[8,896]{1,0:T(8,128)}, f32[2,1024]{1,0:T(2,128)}) custom-call(bf16[16,1024]{1,0:T(8,128)(2,1)} %get-tuple-element.10.refs_0_, bf16[16,1024]{1,0:T(8,128)(2,1)} %get-tuple-element.11.refs_1_, f32[8,896]{1,0:T(8,128)} %get-tuple-element.12.refs_2_, ...), custom_call_target="tpu_custom_call" | custom-call | tf_op jit(solution)/shard_map/pallas_call | solution.py:608

commit v3 on v2

--- a/solution.py
+++ b/solution.py
@@ -45,7 +45,7 @@
     tok, wg, wu, wd, ag, au, ad, bg, bu, bd, cot,
     out, tig, gmap, umap, dmap,
     X, VG, VU, VD, AGU, AD, BGU, BD,
-    LZ, LA, DL, PG, PU, PH, WIDE, GA, UA, RS, RR, H, ST, SB, O2, RX, LOWF,
+    LZ, LA, DL, PS, PG, PU, PH, WIDE, GA, UA, RS, RR, H, ST, SB, O2, RX, LOWF,
     wsem, xsem, xs, xr, vs, vr, ys, yr, lzs, lzr, las, lar, dls, dlr, rss, rsr, ags, agr, sbs, sbr, rxs, rxr,
 ):
     z = lax.axis_index("gx")
@@ -66,11 +66,19 @@
     def sibling_at(i, k):
         return second[i % SIDE] + first[k % SIDE] + 1 - c
 
+    def gray(n):
+        return n + lax.div(n, 2) * (1 - 2 * mod(n, 2))
+
+    def place_of(d, n):
+        return 2 * mod(d + n, 2) + lax.div(n, 2)
+
+    def device_of(d, n):
+        t, step, cc = lax.div(d, 2), gray(n), mod(d + n, 2)
+        across, along = 2 * t + 8 * mod(qy + step, SIDE), 2 * mod(qx + step, SIDE) + 8 * t + 1
+        return across + cc * (along - across)
+
     def owner(d, cc, k):
-        return 4 * mod(d + 4 * cc, NZ) + 2 * k + cc
-
-    def owners(d):
-        return [owner(d, p // 2, p % 2) for p in range(4)]
+        return device_of(d, 2 * k + mod(d + cc, 2))
 
     def remote(src, dst, ssem, rsem, zz, gg):
         return pltpu.make_async_remote_copy(
@@ -78,6 +86,16 @@
         )
 
     me = g
+
+    barrier = pltpu.get_barrier_semaphore()
+
+    @pl.loop(1, NG)
+    def _(k):
+        pl.semaphore_signal(barrier, inc=1, device_id=(z, mod(g + k, NG)), device_id_type=MESH)
+
+    @pl.loop(1, NZ)
+    def _(k):
+        pl.semaphore_signal(barrier, inc=1, device_id=(mod(z + k, NZ), g), device_id_type=MESH)
 
     own_copies = [
         pltpu.make_async_copy(tok, X.at[0, me], xsem.at[0]),
@@ -101,51 +119,30 @@
     for copy in own_copies + low_copies + gate_copies + rest_copies:
         copy.start()
 
-    barrier = pltpu.get_barrier_semaphore()
-
-    @pl.loop(1, NG)
-    def _(k):
-        pl.semaphore_signal(barrier, inc=1, device_id=(z, mod(g + k, NG)), device_id_type=MESH)
-
-    @pl.loop(1, NZ)
-    def _(k):
-        pl.semaphore_signal(barrier, inc=1, device_id=(mod(z + k, NZ), g), device_id_type=MESH)
-
-    zero_half = jnp.zeros((3, CH // 2, FF), BF16)
-    RR[:, 0, 3, CH // 2 : CH, :] = zero_half
-    RR[:, 1, 3, 0 : CH // 2, :] = zero_half
-    RR[:, :, 4] = jnp.zeros((3, 2, CH, FF), BF16)
-    LZ[z] = jnp.zeros((2 * TB, 128), BF16)
-    DL[me] = jnp.zeros((TB, 128), BF16)
-
-    for copy in own_copies:
-        copy.wait()
-
-    for copy in low_copies:
-        copy.wait()
-    LZ[z, 0:TB] = nt(X[0, me], AGU[...]).astype(BF16)
-    LZ[z, TB : 2 * TB, 0:R] = nt(X[1, me], BD[...]).astype(BF16)
-
-
     pl.semaphore_wait(barrier, NG - 1 + NZ - 1)
 
+    def held(a, s):
+        return (tok, cot)[a] if s is me else X.at[a, s]
+
     def near(a, s, i):
-        return remote(X.at[a, s], X.at[a, s], xs.at[a, i], xr.at[a, i], z, device_at(i, 0))
+        return remote(held(a, s), X.at[a, s], xs.at[a, i], xr.at[a, i], z, device_at(i, 0))
 
     def far(a, s, i, k):
-        return remote(X.at[a, s], X.at[a, s], vs.at[a, i, k], vr.at[a, i, k], z, device_at(0, k))
+        return remote(held(a, s), X.at[a, s], vs.at[a, i, k], vr.at[a, i, k], z, device_at(0, k))
 
     def relay(a, s, i, k):
-        return remote(X.at[a, s], X.at[a, s], ys.at[a, i, k], yr.at[a, i, k], z, sibling)
+        return remote(held(a, s), X.at[a, s], ys.at[a, i, k], yr.at[a, i, k], z, sibling)
 
     def spread_near(a):
         for i in (1, 3, 2):
             near(a, me, i).start()
-        relay(a, me, 0, 0).start()
-
-    def spread_turn(a):
+
+    def spread_own(a):
         for k in (1, 3, 2):
             far(a, me, 0, k).start()
+        relay(a, me, 0, 0).start()
+
+    def spread_turn(a):
         for i in (1, 3, 2):
             s = device_at(-i, 0)
             near(a, s, i).wait_recv()
@@ -160,21 +157,35 @@
                 far(a, s, i, k).wait_recv()
                 relay(a, s, i, k).start()
 
-    def spread_wait(a):
-        for k in (0, 3, 1, 2):
+    def spread_wait(a, steps):
+        for k in steps:
             for i in (0, 1, 3, 2):
                 relay(a, sibling_at(-i, -k), i, k).wait_recv()
 
     spread_near(0)
+    spread_own(0)
     spread_near(1)
+
+    RR[:, 0, 3, 2:4] = jnp.zeros((3, 2, TB, FF), BF16)
+    RR[:, 1, 3, 0:2] = jnp.zeros((3, 2, TB, FF), BF16)
+    RR[:, :, 4] = jnp.zeros((3, 2, 4, TB, FF), BF16)
+    LZ[z] = jnp.zeros((2 * TB, 128), BF16)
+    DL[me] = jnp.zeros((TB, 128), BF16)
+
+    for copy in own_copies:
+        copy.wait()
+
+    for copy in low_copies:
+        copy.wait()
+    LZ[z, 0:TB] = nt(X[0, me], AGU[...]).astype(BF16)
+    LZ[z, TB : 2 * TB, 0:R] = nt(X[1, me], BD[...]).astype(BF16)
+
     @pl.loop(1, NZ)
     def _(k):
         remote(LZ.at[z], LZ.at[z], lzs.at[k], lzr.at[k], mod(z + k, NZ), g).start()
 
     spread_turn(0)
-    spread_turn(1)
-    spread_far(0)
-    spread_wait(0)
+    spread_own(1)
 
     def to_plane(ref, ssem, rsem, k):
         return remote(ref.at[me], ref.at[me], ssem.at[k], rsem.at[k], z, mod(g + k, NG))
@@ -200,53 +211,84 @@
         def _(k):
             from_plane(LA, las, lar, k).wait_recv()
 
-    for copy in gate_copies + rest_copies:
-        copy.wait()
-
-    def ring_copy(a, way, j, half):
-        rows = pl.ds(way * (CH // 2), CH // 2) if half else pl.ds(0, CH)
+    def ring_copy(a, way, j, far):
+        at, size = (1, 3) if far else (0, 1)
+        if far and isinstance(j, int) and j == 4:
+            at, size = (2, 2) if way else (1, 1)
+        blocks = pl.ds(at, size)
+        level = far * 4 + j - 1
         return remote(
-            RS.at[a, way, j - 1, rows], RR.at[a, way, j - 1, rows],
-            rss.at[a, way, j - 1], rsr.at[a, way, j - 1], left if way else right, g,
+            RS.at[a, way, j - 1, blocks], RR.at[a, way, j - 1, blocks],
+            rss.at[a, way, level], rsr.at[a, way, level], left if way else right, g,
         )
 
-    def ring_wait(a, j):
+    def ring_wait(a, j, far):
         @pl.when(j == 3)
         def _():
-            ring_copy(a, 0, 4, True).wait_recv()
-            ring_copy(a, 1, 4, True).wait_recv()
+            ring_copy(a, 0, 4, far).wait_recv()
+            if far:
+                ring_copy(a, 1, 4, far).wait_recv()
 
         @pl.when(j < 3)
         def _():
-            ring_copy(a, 0, j + 1, False).wait_recv()
-            ring_copy(a, 1, j + 1, False).wait_recv()
+            ring_copy(a, 0, j + 1, far).wait_recv()
+            ring_copy(a, 1, j + 1, far).wait_recv()
+
+    def ring_send(a, j, far):
+        @pl.when(j == 4)
+        def _():
+            ring_copy(a, 0, 4, far).start()
+            if far:
+                ring_copy(a, 1, 4, far).start()
+
+        @pl.when((j > 0) & (j < 4))
+        def _():
+            ring_copy(a, 0, j, far).start()
+            ring_copy(a, 1, j, far).start()
+
+    def near_products(a, x, weight):
+        PS[a] = weight(x).reshape(NZ, TB, FF)
+        RS[a, 0, 3, 0] = PS[a, mod(z + 4, NZ)].astype(BF16)
+        ring_copy(a, 0, 4, False).start()
+
+    def near_step(a, j):
+        ring_wait(a, j, False)
+
+        @pl.when(j > 0)
+        def _():
+            for way, d in ((0, mod(z + j, NZ)), (1, mod(z + NZ - j, NZ))):
+                RS[a, way, j - 1, 0] = (PS[a, d] + RR[a, way, j, 0].astype(F32)).astype(BF16)
+
+        ring_send(a, j, False)
+
+    def near_group(a):
+        return jnp.concatenate([X[a, device_of(d, 0)] for d in range(NZ)], axis=0)
 
     def pair(a, j):
-        return jnp.concatenate([X[a, p] for d in (mod(z + j, NZ), mod(z + NZ - j, NZ)) for p in owners(d)], axis=0)
+        chunks = (mod(z + j, NZ), mod(z + NZ - j, NZ))
+        return jnp.concatenate([X[a, device_of(d, n)] for d in chunks for n in (1, 2, 3)], axis=0)
 
     def ring_step(a, part, j):
-        ring_wait(a, j)
+        ring_wait(a, j, True)
 
         @pl.when(j > 0)
         def _():
-            RS[a, 0, j - 1] = (part[0:CH] + RR[a, 0, j].astype(F32)).astype(BF16)
-            RS[a, 1, j - 1] = (part[CH : 2 * CH] + RR[a, 1, j].astype(F32)).astype(BF16)
-
-        @pl.when(j == 4)
-        def _():
-            ring_copy(a, 0, 4, True).start()
-            ring_copy(a, 1, 4, True).start()
-
-        @pl.when((j > 0) & (j < 4))
-        def _():
-            ring_copy(a, 0, j, False).start()
-            ring_copy(a, 1, j, False).start()
+            for way in range(2):
+                total = part[way * 3 * TB : (way + 1) * 3 * TB].reshape(3, TB, FF) + RR[a, way, j, 1:4].astype(F32)
+                RS[a, way, j - 1, 1:4] = total.astype(BF16)
+
+        ring_send(a, j, True)
 
     def ring_total(a, part):
-        return part[0:CH] + (RR[a, 0, 0].astype(F32) + RR[a, 1, 0].astype(F32))
+        own = jnp.concatenate([PS[a, z], part[0 : 3 * TB]], axis=0)
+        return own + (RR[a, 0, 0].astype(F32) + RR[a, 1, 0].astype(F32)).reshape(CH, FF)
 
     def low_chunk(which):
-        return jnp.concatenate([LA[p, which * TB : (which + 1) * TB] for p in owners(z)], axis=0)
+        return jnp.concatenate([LA[device_of(z, n), which * TB : (which + 1) * TB] for n in range(4)], axis=0)
+
+    def put_chunk(b, value):
+        for n in range(4):
+            H[b, z, place_of(z, n)] = value[n * TB : (n + 1) * TB].astype(BF16)
 
     def half_rows(low, first):
         lane = lax.broadcasted_iota(jnp.int32, low.shape, 1)
@@ -255,9 +297,9 @@
     def chain_copy(b, way, j, half, arriving):
         hops = j if arriving else j - 1
         d = mod(z + hops, NZ) if way else mod(z + NZ - hops, NZ)
-        rows = pl.ds(way * (CH // 2), CH // 2) if half else pl.ds(0, CH)
+        blocks = pl.ds(2 * way, 2) if half else pl.ds(0, 4)
         return remote(
-            H.at[b, d, rows], H.at[b, d, rows],
+            H.at[b, d, blocks], H.at[b, d, blocks],
             ags.at[b, way, j - 1], agr.at[b, way, j - 1], left if way else right, g,
         )
 
@@ -282,6 +324,25 @@
         def _():
             chain_copy(b, 0, j, False, True).wait_recv()
             chain_copy(b, 1, j, False, True).wait_recv()
+
+    spread_wait(0, (0,))
+    for copy in gate_copies:
+        copy.wait()
+    x = near_group(0)
+    near_products(0, x, lambda x: nn(x, VG[...]))
+    near_products(1, x, lambda x: nn(x, VU[...]))
+    spread_turn(1)
+    spread_wait(1, (0,))
+    for copy in rest_copies:
+        copy.wait()
+    near_products(2, near_group(1), lambda x: nt(x, VD[...]))
+    spread_far(0)
+
+    @pl.loop(0, 2)
+    def _(a):
+        near_step(a, 3)
+
+    spread_wait(0, (3, 1, 2))
 
     @pl.loop(0, 6)
     def _(i):
@@ -302,16 +363,25 @@
                 up = ring_total(1, PU) + SCALE * nn(half_rows(low, False), BGU[...])
                 GA[...] = gate
                 UA[...] = up
-                H[0, z] = (gate * jax.nn.sigmoid(gate) * up).astype(BF16)
+                put_chunk(0, gate * jax.nn.sigmoid(gate) * up)
                 chain_start(0, 1)
 
+        @pl.when(i < 3)
+        def _():
+            near_step(0, 2 - i)
+            near_step(1, 2 - i)
+
+        @pl.when(i < 4)
+        def _():
+            near_step(2, 3 - i)
+
         @pl.when(i == 0)
         def _():
             spread_far(1)
 
         @pl.when(i == 1)
         def _():
-            spread_wait(1)
+            spread_wait(1, (3, 1, 2))
 
         @pl.when(i == 5)
         def _():
@@ -329,9 +399,9 @@
                 grad = ring_total(2, PH) + SCALE * nn(low_chunk(1)[:, 0:R], AD[...])
                 gate, up = GA[...], UA[...]
                 sigma = jax.nn.sigmoid(gate)
-                H[1, z] = (grad * up * sigma * (1.0 + gate * (1.0 - sigma))).astype(BF16)
+                put_chunk(1, grad * up * sigma * (1.0 + gate * (1.0 - sigma)))
                 chain_start(1, 1)
-                H[2, z] = (grad * gate * sigma).astype(BF16)
+                put_chunk(2, grad * gate * sigma)
                 chain_start(2, 1)
 
         @pl.when(i == 1)
@@ -380,10 +450,13 @@
             combine_one(f, mod(z + j, NZ))
 
     def hpair(b, j):
-        return jnp.concatenate([H[b, mod(z + NZ - j, NZ)], H[b, mod(z + j, NZ)]], axis=0)
+        return jnp.concatenate([H[b, d].reshape(CH, FF) for d in (mod(z + NZ - j, NZ), mod(z + j, NZ))], axis=0)
 
     def adapter_grads(b, j, x):
-        low = jnp.concatenate([LA[p, 0:TB] for d in (mod(z + NZ - j, NZ), mod(z + j, NZ)) for p in owners(d)], axis=0)
+        da, db = mod(z + NZ - j, NZ), mod(z + j, NZ)
+        low = [LA[device_of(d, n), 0:TB] for d in (da, db) for n in (0, 2, 1, 3)]
+        low = [jnp.where(mod(d, 2) == 0, low[4 * m + i], low[4 * m + (i + 2) % 4]) for m, d in enumerate((da, db)) for i in range(4)]
+        low = jnp.concatenate(low, axis=0)
         once = (lax.broadcasted_iota(jnp.int32, (2 * CH, 128), 0) < CH) | (mod(j, 4) > 0)
         LOWF[b] += tn(jnp.where(once, low, jnp.zeros_like(low)), x)
 
@@ -489,11 +562,11 @@
         to_plane(LA, las, lar, k).wait_send()
 
     for a in range(3):
+        ring_copy(a, 0, 4, False).wait_send()
         for way in range(2):
             ring_copy(a, way, 4, True).wait_send()
-
-            @pl.loop(1, 4)
-            def _(j):
+            for j in range(1, 4):
+                ring_copy(a, way, j, True).wait_send()
                 ring_copy(a, way, j, False).wait_send()
 
     @pl.loop(1, NG)
@@ -505,10 +578,6 @@
     for k in range(2):
         dmap[k : k + 1] = jnp.sum(jnp.where(rank == 2 * g + k, grads, 0.0), axis=0, keepdims=True)
 
-    total = rows_total(1)
-    back = total[:, D:W].astype(BF16)
-    tig[...] = (total[:, 0:D] + SCALE * nn(back, AGU[...])).astype(BF16)
-
     @pl.loop(1, NG)
     def _(k):
         to_plane(DL, dls, dlr, k).wait_send()
@@ -516,19 +585,29 @@
     for a in range(3):
         for way in range(2):
             chain_copy(a, way, 4, True, False).wait_send()
-
-            @pl.loop(1, 4)
-            def _(j):
+            for j in range(1, 4):
                 chain_copy(a, way, j, False, False).wait_send()
+
+    def owner_sent(f, d):
+        for k in range(2):
+            @pl.when(owner(d, c, k) != g)
+            def _():
+                owner_copy(f, d, k).wait_send()
 
     @pl.loop(0, NZ)
     def _(d):
         for f in range(2):
             sib_copy(f, d).wait_send()
-            for k in range(2):
-                @pl.when(owner(d, c, k) != g)
-                def _():
-                    owner_copy(f, d, k).wait_send()
+        owner_sent(0, d)
+
+        @pl.when(d != mod(z + 4, NZ))
+        def _():
+            owner_sent(1, d)
+
+    total = rows_total(1)
+    back = total[:, D:W].astype(BF16)
+    tig[...] = (total[:, 0:D] + SCALE * nn(back, AGU[...])).astype(BF16)
+    owner_sent(1, mod(z + 4, NZ))
 
 
 def place(*refs):
@@ -564,15 +643,16 @@
             pltpu.VMEM((NZ, 2 * TB, 128), BF16),
             pltpu.VMEM((NG, 2 * TB, 128), BF16),
             pltpu.VMEM((NG, TB, 128), BF16),
-            pltpu.VMEM((2 * CH, FF), F32),
-            pltpu.VMEM((2 * CH, FF), F32),
-            pltpu.VMEM((2 * CH, FF), F32),
+            pltpu.VMEM((3, NZ, TB, FF), F32),
+            pltpu.VMEM((6 * TB, FF), F32),
+            pltpu.VMEM((6 * TB, FF), F32),
+            pltpu.VMEM((6 * TB, FF), F32),
             pltpu.VMEM((2 * CH, W), F32),
             pltpu.VMEM((CH, FF), F32),
             pltpu.VMEM((CH, FF), F32),
-            pltpu.VMEM((3, 2, 4, CH, FF), BF16),
-            pltpu.VMEM((3, 2, 5, CH, FF), BF16),
-            pltpu.VMEM((3, NZ, CH, FF), BF16),
+            pltpu.VMEM((3, 2, 4, 4, TB, FF), BF16),
+            pltpu.VMEM((3, 2, 5, 4, TB, FF), BF16),
+            pltpu.VMEM((3, NZ, 4, TB, FF), BF16),
             pltpu.VMEM((2, NZ, CH, W), BF16),
             pltpu.VMEM((2, NZ, CH // 2, W), BF16),
             pltpu.VMEM((2, NZ, CH // 2, W), BF16),
@@ -592,8 +672,8 @@
             dma((NG,)),
             dma((NG,)),
             dma((NG,)),
-            dma((3, 2, 4)),
-            dma((3, 2, 4)),
+            dma((3, 2, 8)),
+            dma((3, 2, 8)),
             dma((3, 2, 4)),
             dma((3, 2, 4)),
             dma((2, NZ)),

time: 94.9 us -> 91.9 us (0.968)
  Pallas kernels: 94.1 us -> 91.1 us
    pallas_call x1, Pallas kernels: 92.7 us -> 89.6 us  [body(): pl.pallas_call(kernel, out_shape=(jax.ShapeDtypeStruct((TB, D), BF16), ja...]
where the time goes in v3:
time: 91.9 us; the launch traced here: 91.7 us
  Pallas kernels  91.1 us (99%)
    pallas_call x1, Pallas kernels, body(): pl.pallas_call(kernel, out_shape=(jax.ShapeDtypeStruct((TB, D), BF16), ja...  89.6 us

profile of v3, /device:TPU:1, one launch (start us, length us, event | category | flops | bytes accessed | tf_op | source)
XLA Modules:
  0.0 91.7 jit_solution(9025641533863912723)
XLA Ops:
  0.6 89.6 %shard_map.146 = (bf16[16,1024]{1,0:T(8,128)(2,1)}, bf16[16,1024]{1,0:T(8,128)(2,1)}, f32[8,896]{1,0:T(8,128)}, f32[8,896]{1,0:T(8,128)}, f32[2,1024]{1,0:T(2,128)}) custom-call(bf16[16,1024]{1,0:T(8,128)(2,1)} %tok.1, bf16[1024,896]{1,0:T(8,128)(2,1)} %wg.1, bf16[1024,896]{1,0:T(8,128)(2,1)} %wu.1, bf16[896,1024]{1,0:T(8,128)(2,1)} %wd.1, ...), custom_call_target="tpu_custom_call" | custom-call | tf_op jit(solution)/shard_map/pallas_call | solution.py:623
  90.3 1.4 %shard_map.147 = (bf16[16,1024]{1,0:T(8,128)(2,1)}, bf16[16,1024]{1,0:T(8,128)(2,1)}, f32[8,896]{1,0:T(8,128)}, f32[8,896]{1,0:T(8,128)}, f32[2,1024]{1,0:T(2,128)}) custom-call(bf16[16,1024]{1,0:T(8,128)(2,1)} %get-tuple-element.10.refs_0_, bf16[16,1024]{1,0:T(8,128)(2,1)} %get-tuple-element.11.refs_1_, f32[8,896]{1,0:T(8,128)} %get-tuple-element.12.refs_2_, ...), custom_call_target="tpu_custom_call" | custom-call | tf_op jit(solution)/shard_map/pallas_call | solution.py:688

commit v4 on v3

--- a/solution.py
+++ b/solution.py
@@ -89,9 +89,9 @@
 
     barrier = pltpu.get_barrier_semaphore()
 
-    @pl.loop(1, NG)
-    def _(k):
-        pl.semaphore_signal(barrier, inc=1, device_id=(z, mod(g + k, NG)), device_id_type=MESH)
+    partners = [sibling] + [device_at(i, 0) for i in (1, 2, 3)] + [device_at(0, k) for k in (1, 2, 3)]
+    for p in partners:
+        pl.semaphore_signal(barrier, inc=1, device_id=(z, p), device_id_type=MESH)
 
     @pl.loop(1, NZ)
     def _(k):
@@ -119,7 +119,7 @@
     for copy in own_copies + low_copies + gate_copies + rest_copies:
         copy.start()
 
-    pl.semaphore_wait(barrier, NG - 1 + NZ - 1)
+    pl.semaphore_wait(barrier, len(partners) + NZ - 1)
 
     def held(a, s):
         return (tok, cot)[a] if s is me else X.at[a, s]
@@ -511,7 +511,6 @@
             x = hpair(1, j)
             WIDE[:, 0:D] = nt(x, VG[...])
             WIDE[:, D:W] = nt(x, BGU[...])
-            adapter_grads(0, j, x)
 
         @pl.when(u < 5)
         def _():
@@ -538,6 +537,7 @@
             stage(1, j, WIDE[:, 0:D] + nt(x, VU[...]), low, 128)
             sib_start(1, j)
             adapter_grads(1, j, x)
+            adapter_grads(0, j, hpair(1, j))
 
     for b, ref in ((0, gmap), (1, umap)):
         ref[...] = SCALE * LOWF[b, pl.ds(pl.multiple_of(R * b + 8 * z, 8), 8)]

time: 91.9 us -> 91.2 us (level)
  no operation moved by 1% of the time
where the time goes in v4:
time: 91.2 us; the launch traced here: 91.1 us
  Pallas kernels  90.4 us (99%)
    pallas_call x1, Pallas kernels, body(): pl.pallas_call(kernel, out_shape=(jax.ShapeDtypeStruct((TB, D), BF16), ja...  89 us

profile of v4, /device:TPU:1, one launch (start us, length us, event | category | flops | bytes accessed | tf_op | source)
XLA Modules:
  0.0 91.1 jit_solution(9579057732419785273)
XLA Ops:
  0.6 89.0 %shard_map.146 = (bf16[16,1024]{1,0:T(8,128)(2,1)}, bf16[16,1024]{1,0:T(8,128)(2,1)}, f32[8,896]{1,0:T(8,128)}, f32[8,896]{1,0:T(8,128)}, f32[2,1024]{1,0:T(2,128)}) custom-call(bf16[16,1024]{1,0:T(8,128)(2,1)} %tok.1, bf16[1024,896]{1,0:T(8,128)(2,1)} %wg.1, bf16[1024,896]{1,0:T(8,128)(2,1)} %wu.1, bf16[896,1024]{1,0:T(8,128)(2,1)} %wd.1, ...), custom_call_target="tpu_custom_call" | custom-call | tf_op jit(solution)/shard_map/pallas_call | solution.py:623
  89.6 1.4 %shard_map.147 = (bf16[16,1024]{1,0:T(8,128)(2,1)}, bf16[16,1024]{1,0:T(8,128)(2,1)}, f32[8,896]{1,0:T(8,128)}, f32[8,896]{1,0:T(8,128)}, f32[2,1024]{1,0:T(2,128)}) custom-call(bf16[16,1024]{1,0:T(8,128)(2,1)} %get-tuple-element.10.refs_0_, bf16[16,1024]{1,0:T(8,128)(2,1)} %get-tuple-element.11.refs_1_, f32[8,896]{1,0:T(8,128)} %get-tuple-element.12.refs_2_, ...), custom_call_target="tpu_custom_call" | custom-call | tf_op jit(solution)/shard_map/pallas_call | solution.py:688
